TPU v7x, 32 devices: a whole 2x2x4 slice. The times are simulated.
32 devices in a mesh: seq: 4 (over y, x), ctx: 8 (over z, core).
Axes of the slice: x: 2, y: 2, z: 4, core: 2. Of those that a mesh axis runs over, the one named last changes fastest.
Arguments:
- tokens: bfloat16 [4, 4096, 768], P('seq', 'ctx'), may hold values from -6 to 6
- segment_ids: int32 [4, 4096], P('seq', 'ctx'), may hold values from 0 to 34, as said below
- valid_tokens: int32 [4, 4096], P('seq', 'ctx'), may hold values from 0 to 1, as said below
- query_weight: float32 [768, 768], P(('seq', 'ctx')), may hold values from -0.21875 to 0.21875
- query_bias: float32 [768], P(('seq', 'ctx')), may hold values from -1.75 to 1.75
- key_weight: float32 [768, 768], P(('seq', 'ctx')), may hold values from -0.21875 to 0.21875
- value_weight: float32 [768, 768], P(('seq', 'ctx')), may hold values from -0.21875 to 0.21875
- value_bias: float32 [768], P(('seq', 'ctx')), may hold values from -1.75 to 1.75
- output_weight: float32 [768, 768], P(('seq', 'ctx')), may hold values from -0.875 to 0.875
- output_bias: float32 [768], P(('seq', 'ctx')), may hold values from -1.75 to 1.75
- attn_norm_gain: float32 [768], P(('seq', 'ctx')), may hold values from 0.5 to 1.5
- attn_norm_shift: float32 [768], P(('seq', 'ctx')), may hold values from -1.75 to 1.75
- up_weight: float32 [768, 3072], P(('seq', 'ctx')), may hold values from -0.21875 to 0.21875
- up_bias: float32 [3072], P(('seq', 'ctx')), may hold values from -1.75 to 1.75
- down_weight: float32 [3072, 768], P(('seq', 'ctx')), may hold values from -0.109375 to 0.109375
- down_bias: float32 [768], P(('seq', 'ctx')), may hold values from -1.75 to 1.75
- ffn_norm_gain: float32 [768], P(('seq', 'ctx')), may hold values from 0.5 to 1.5
- ffn_norm_shift: float32 [768], P(('seq', 'ctx')), may hold values from -1.75 to 1.75
- out_cotangent: bfloat16 [4, 4096, 768], P('seq', 'ctx'), may hold values from -6 to 6
Outputs:
- layer_output: float32 [4, 4096, 768], P('seq', 'ctx')
- input_grad: float32 [4, 4096, 768], P('seq', 'ctx')
- query_weight_grad: float32 [768, 768], P(('seq', 'ctx'))
- query_bias_grad: float32 [768], P(('seq', 'ctx'))
- key_weight_grad: float32 [768, 768], P(('seq', 'ctx'))
- value_weight_grad: float32 [768, 768], P(('seq', 'ctx'))
- value_bias_grad: float32 [768], P(('seq', 'ctx'))
- output_weight_grad: float32 [768, 768], P(('seq', 'ctx'))
- output_bias_grad: float32 [768], P(('seq', 'ctx'))
- attn_norm_gain_grad: float32 [768], P(('seq', 'ctx'))
- attn_norm_shift_grad: float32 [768], P(('seq', 'ctx'))
- up_weight_grad: float32 [768, 3072], P(('seq', 'ctx'))
- up_bias_grad: float32 [3072], P(('seq', 'ctx'))
- down_weight_grad: float32 [3072, 768], P(('seq', 'ctx'))
- down_bias_grad: float32 [768], P(('seq', 'ctx'))
- ffn_norm_gain_grad: float32 [768], P(('seq', 'ctx'))
- ffn_norm_shift_grad: float32 [768], P(('seq', 'ctx'))
Inputs may be any that keep to these rules, and one draw needn't show every extreme that they name: `segment_ids`: within each sequence the numbers start at 0 and rise by 0 or 1 from one token to the next, so that documents are contiguous; every sequence holds exactly 35 documents. `valid_tokens`: each sequence ends in a run of padding; the first token of every document is 1.
All inputs are finite; a program needn't handle non-finite values.
Results may differ from a plain program's by a relative error of at most 0.025.
Values may be sent and summed in bfloat16 or wider, within the bound.
A program may use at most 192 MiB of HBM per device.

v0:
```python
from functools import partial

import jax
import jax.numpy as jnp
from jax import lax
from jax.sharding import PartitionSpec as P

H = 12
DH = 64


epsilon = 1e-12


def layer_norm(hidden, gain, shift):
    centred = hidden - jnp.mean(hidden, axis=-1, keepdims=True)
    variance = jnp.mean(centred * centred, axis=-1, keepdims=True)
    return centred * lax.rsqrt(variance + epsilon) * gain + shift


def column_sum(values):
    return jnp.sum(values.astype(jnp.float32), axis=0)


def score_block(query_heads, key_heads, query_codes, key_codes):
    scores = jnp.einsum(
        "qhd,khd->qhk", query_heads, key_heads, preferred_element_type=jnp.float32
    ) * DH ** (-0.5)
    allowed = (key_codes[None, :] == query_codes[:, None])[:, None, :]
    return jnp.where(allowed, scores, -1e30)


def block_grads(
    query_heads, grad_heads, row_lse, row_delta, query_codes, key_heads, value_heads, key_codes
):
    scores = score_block(query_heads, key_heads, query_codes, key_codes)
    probability = jnp.exp(scores - row_lse[:, :, None])
    grad_prob = jnp.einsum(
        "qhd,khd->qhk", grad_heads, value_heads, preferred_element_type=jnp.float32
    )
    grad_scores = (probability * (grad_prob - row_delta[:, :, None])).astype(jnp.bfloat16)
    score_scale = DH ** (-0.5)
    grad_query = (
        jnp.einsum("qhk,khd->qhd", grad_scores, key_heads, preferred_element_type=jnp.float32)
        * score_scale
    )
    grad_key = (
        jnp.einsum("qhk,qhd->khd", grad_scores, query_heads, preferred_element_type=jnp.float32)
        * score_scale
    )
    grad_value = jnp.einsum(
        "qhk,qhd->khd",
        probability.astype(jnp.bfloat16),
        grad_heads,
        preferred_element_type=jnp.float32,
    )
    return (grad_query, grad_key, grad_value)


def on_device(
    tokens,
    segment_ids,
    valid_tokens,
    query_weight,
    query_bias,
    key_weight,
    value_weight,
    value_bias,
    output_weight,
    output_bias,
    attn_norm_gain,
    attn_norm_shift,
    up_weight,
    up_bias,
    down_weight,
    down_bias,
    ffn_norm_gain,
    ffn_norm_shift,
    out_cotangent,
):
    gathered = (
        lax.all_gather(query_weight.astype(jnp.bfloat16), ("seq", "ctx"), axis=0, tiled=True),
        lax.all_gather(query_bias.astype(jnp.bfloat16), ("seq", "ctx"), axis=0, tiled=True),
        lax.all_gather(key_weight.astype(jnp.bfloat16), ("seq", "ctx"), axis=0, tiled=True),
        lax.all_gather(value_weight.astype(jnp.bfloat16), ("seq", "ctx"), axis=0, tiled=True),
        lax.all_gather(value_bias.astype(jnp.bfloat16), ("seq", "ctx"), axis=0, tiled=True),
        lax.all_gather(output_weight.astype(jnp.bfloat16), ("seq", "ctx"), axis=0, tiled=True),
        lax.all_gather(output_bias.astype(jnp.bfloat16), ("seq", "ctx"), axis=0, tiled=True),
        lax.all_gather(attn_norm_gain.astype(jnp.bfloat16), ("seq", "ctx"), axis=0, tiled=True),
        lax.all_gather(attn_norm_shift.astype(jnp.bfloat16), ("seq", "ctx"), axis=0, tiled=True),
        lax.all_gather(up_weight.astype(jnp.bfloat16), ("seq", "ctx"), axis=0, tiled=True),
        lax.all_gather(up_bias.astype(jnp.bfloat16), ("seq", "ctx"), axis=0, tiled=True),
        lax.all_gather(down_weight.astype(jnp.bfloat16), ("seq", "ctx"), axis=0, tiled=True),
        lax.all_gather(down_bias.astype(jnp.bfloat16), ("seq", "ctx"), axis=0, tiled=True),
        lax.all_gather(ffn_norm_gain.astype(jnp.bfloat16), ("seq", "ctx"), axis=0, tiled=True),
        lax.all_gather(ffn_norm_shift.astype(jnp.bfloat16), ("seq", "ctx"), axis=0, tiled=True),
    )
    (
        proj_query,
        bias_query,
        proj_key,
        proj_value,
        bias_value,
        proj_output,
        bias_output,
        gain_attn,
        shift_attn,
        proj_up,
        bias_up,
        proj_down,
        bias_down,
        gain_ffn,
        shift_ffn,
    ) = gathered
    inputs = tokens[0]
    local_rows = inputs.shape[0]
    model_width = inputs.shape[1]
    token_codes = segment_ids[0] * 2 + valid_tokens[0]
    targets = token_codes // 2 * 2 + 1
    key_codes = lax.all_gather(token_codes, "ctx", axis=0, tiled=True)
    queries = (
        jnp.dot(inputs, proj_query, preferred_element_type=jnp.float32)
        + bias_query.astype(jnp.float32)
    ).astype(jnp.bfloat16)
    key_rows = jnp.dot(inputs, proj_key, preferred_element_type=jnp.float32).astype(jnp.bfloat16)
    values = (
        jnp.dot(inputs, proj_value, preferred_element_type=jnp.float32)
        + bias_value.astype(jnp.float32)
    ).astype(jnp.bfloat16)
    query_heads = queries.reshape(local_rows, H, DH)
    start_state = (
        jnp.full((local_rows, H), -1e30, jnp.float32),
        jnp.zeros((local_rows, H), jnp.float32),
        jnp.zeros((local_rows, H, DH), jnp.float32),
    )
    key_piece = lax.all_gather(key_rows, "ctx", axis=0, tiled=True)
    value_piece = lax.all_gather(values, "ctx", axis=0, tiled=True)
    row_count = key_piece.shape[0]
    block_rows = min(512, row_count)

    def attend_inner(block_index, inner_state):
        running_max, running_sum, weighted = inner_state
        offset = block_index * block_rows
        key_block = lax.dynamic_slice_in_dim(key_piece, offset, block_rows, 0).reshape(
            block_rows, H, DH
        )
        value_block = lax.dynamic_slice_in_dim(value_piece, offset, block_rows, 0).reshape(
            block_rows, H, DH
        )
        code_block = lax.dynamic_slice_in_dim(key_codes, offset, block_rows, 0)
        scores = score_block(query_heads, key_block, targets, code_block)
        new_max = jnp.maximum(running_max, jnp.max(scores, axis=-1))
        probability = jnp.exp(scores - new_max[:, :, None])
        fading = jnp.exp(running_max - new_max)
        running_sum = running_sum * fading + jnp.sum(probability, axis=-1)
        weighted = weighted * fading[:, :, None] + jnp.einsum(
            "qhk,khd->qhd",
            probability.astype(jnp.bfloat16),
            value_block,
            preferred_element_type=jnp.float32,
        )
        return (new_max, running_sum, weighted)

    running_max, running_sum, weighted = lax.fori_loop(
        0, row_count // block_rows, attend_inner, start_state
    )
    row_lse = running_max + jnp.log(running_sum)
    mixed_float = weighted / running_sum[:, :, None]
    mixed_rows = mixed_float.reshape(local_rows, model_width).astype(jnp.bfloat16)
    attended = jnp.dot(
        mixed_rows, proj_output, preferred_element_type=jnp.float32
    ) + bias_output.astype(jnp.float32)
    inputs_float = inputs.astype(jnp.float32)
    normed_attn, norm_back_one = jax.vjp(
        layer_norm,
        inputs_float + attended,
        gain_attn.astype(jnp.float32),
        shift_attn.astype(jnp.float32),
    )
    normed_low = normed_attn.astype(jnp.bfloat16)
    hidden = jnp.dot(normed_low, proj_up, preferred_element_type=jnp.float32) + bias_up.astype(
        jnp.float32
    )
    activated, gelu_back = jax.vjp(partial(jax.nn.gelu, approximate=False), hidden)
    activated_low = activated.astype(jnp.bfloat16)
    branch = jnp.dot(
        activated_low, proj_down, preferred_element_type=jnp.float32
    ) + bias_down.astype(jnp.float32)
    output, norm_back_two = jax.vjp(
        layer_norm,
        normed_attn + branch,
        gain_ffn.astype(jnp.float32),
        shift_ffn.astype(jnp.float32),
    )
    grad_second, grad_gain_ffn, grad_shift_ffn = norm_back_two(out_cotangent[0].astype(jnp.float32))
    grad_branch = grad_second.astype(jnp.bfloat16)
    grad_bias_down = column_sum(grad_branch)
    grad_proj_down = jnp.einsum(
        "tf,td->fd", activated_low, grad_branch, preferred_element_type=jnp.float32
    )
    grad_activated = jnp.einsum(
        "td,fd->tf", grad_branch, proj_down, preferred_element_type=jnp.float32
    )
    grad_hidden = gelu_back(grad_activated)[0].astype(jnp.bfloat16)
    grad_bias_up = column_sum(grad_hidden)
    grad_proj_up = jnp.einsum(
        "td,tf->df", normed_low, grad_hidden, preferred_element_type=jnp.float32
    )
    grad_normed = grad_second + jnp.einsum(
        "tf,df->td", grad_hidden, proj_up, preferred_element_type=jnp.float32
    )
    grad_resid, grad_gain_attn, grad_shift_attn = norm_back_one(grad_normed)
    grad_attended = grad_resid.astype(jnp.bfloat16)
    grad_bias_output = column_sum(grad_attended)
    grad_proj_output = jnp.einsum(
        "td,te->de", mixed_rows, grad_attended, preferred_element_type=jnp.float32
    )
    grad_mixed = jnp.einsum(
        "te,de->td", grad_attended, proj_output, preferred_element_type=jnp.float32
    ).astype(jnp.bfloat16)
    grad_heads = grad_mixed.reshape(local_rows, H, DH)
    row_delta = jnp.sum(grad_heads.astype(jnp.float32) * mixed_float, axis=-1)
    query_start = jnp.zeros((local_rows, H, DH), jnp.float32)
    total_rows = lax.axis_size("ctx") * local_rows
    grads_key_piece = lax.all_gather(key_rows, "ctx", axis=0, tiled=True)
    grads_value_piece = lax.all_gather(values, "ctx", axis=0, tiled=True)
    row_count = grads_key_piece.shape[0]
    grads_block_rows = min(512, row_count)

    def grads_inner(block_index, inner_state):
        query_total, pair_total = inner_state
        offset = block_index * grads_block_rows
        key_block = lax.dynamic_slice_in_dim(grads_key_piece, offset, grads_block_rows, 0).reshape(
            grads_block_rows, H, DH
        )
        value_block = lax.dynamic_slice_in_dim(
            grads_value_piece, offset, grads_block_rows, 0
        ).reshape(grads_block_rows, H, DH)
        code_block = lax.dynamic_slice_in_dim(key_codes, offset, grads_block_rows, 0)
        part_query, part_key, part_value = block_grads(
            query_heads, grad_heads, row_lse, row_delta, targets, key_block, value_block, code_block
        )
        joined = jnp.concatenate(
            [
                part_key.reshape(grads_block_rows, model_width),
                part_value.reshape(grads_block_rows, model_width),
            ],
            axis=1,
        )
        return (
            query_total + part_query,
            lax.dynamic_update_slice_in_dim(pair_total, joined, offset, 0),
        )

    grad_query, grad_pairs = lax.fori_loop(
        0,
        row_count // grads_block_rows,
        grads_inner,
        (query_start, jnp.zeros((total_rows, 2 * model_width), jnp.float32)),
    )
    owned = lax.psum_scatter(
        grad_pairs.astype(jnp.bfloat16), "ctx", scatter_dimension=0, tiled=True
    ).astype(jnp.float32)
    grad_keys = owned[:, :model_width].astype(jnp.bfloat16)
    grad_values = owned[:, model_width:].astype(jnp.bfloat16)
    grad_queries = grad_query.reshape(local_rows, model_width).astype(jnp.bfloat16)
    grad_proj_query = jnp.einsum(
        "td,te->de", inputs, grad_queries, preferred_element_type=jnp.float32
    )
    grad_bias_query = column_sum(grad_queries)
    grad_proj_key = jnp.einsum("td,te->de", inputs, grad_keys, preferred_element_type=jnp.float32)
    grad_proj_value = jnp.einsum(
        "td,te->de", inputs, grad_values, preferred_element_type=jnp.float32
    )
    grad_bias_value = column_sum(grad_values)
    grad_inputs = (
        grad_resid
        + jnp.einsum("te,de->td", grad_queries, proj_query, preferred_element_type=jnp.float32)
        + jnp.einsum("te,de->td", grad_keys, proj_key, preferred_element_type=jnp.float32)
        + jnp.einsum("te,de->td", grad_values, proj_value, preferred_element_type=jnp.float32)
    )
    summed = (
        lax.psum_scatter(grad_proj_query, ("seq", "ctx"), scatter_dimension=0, tiled=True),
        lax.psum_scatter(grad_bias_query, ("seq", "ctx"), scatter_dimension=0, tiled=True),
        lax.psum_scatter(grad_proj_key, ("seq", "ctx"), scatter_dimension=0, tiled=True),
        lax.psum_scatter(grad_proj_value, ("seq", "ctx"), scatter_dimension=0, tiled=True),
        lax.psum_scatter(grad_bias_value, ("seq", "ctx"), scatter_dimension=0, tiled=True),
        lax.psum_scatter(grad_proj_output, ("seq", "ctx"), scatter_dimension=0, tiled=True),
        lax.psum_scatter(grad_bias_output, ("seq", "ctx"), scatter_dimension=0, tiled=True),
        lax.psum_scatter(grad_gain_attn, ("seq", "ctx"), scatter_dimension=0, tiled=True),
        lax.psum_scatter(grad_shift_attn, ("seq", "ctx"), scatter_dimension=0, tiled=True),
        lax.psum_scatter(grad_proj_up, ("seq", "ctx"), scatter_dimension=0, tiled=True),
        lax.psum_scatter(grad_bias_up, ("seq", "ctx"), scatter_dimension=0, tiled=True),
        lax.psum_scatter(grad_proj_down, ("seq", "ctx"), scatter_dimension=0, tiled=True),
        lax.psum_scatter(grad_bias_down, ("seq", "ctx"), scatter_dimension=0, tiled=True),
        lax.psum_scatter(grad_gain_ffn, ("seq", "ctx"), scatter_dimension=0, tiled=True),
        lax.psum_scatter(grad_shift_ffn, ("seq", "ctx"), scatter_dimension=0, tiled=True),
    )
    return (
        output[None],
        grad_inputs[None],
        summed[0],
        summed[1],
        summed[2],
        summed[3],
        summed[4],
        summed[5],
        summed[6],
        summed[7],
        summed[8],
        summed[9],
        summed[10],
        summed[11],
        summed[12],
        summed[13],
        summed[14],
    )


def solution(mesh):
    in_specs = (
        P("seq", "ctx", None),
        P("seq", "ctx"),
        P("seq", "ctx"),
        P(("seq", "ctx"), None),
        P(("seq", "ctx")),
        P(("seq", "ctx"), None),
        P(("seq", "ctx"), None),
        P(("seq", "ctx")),
        P(("seq", "ctx"), None),
        P(("seq", "ctx")),
        P(("seq", "ctx")),
        P(("seq", "ctx")),
        P(("seq", "ctx"), None),
        P(("seq", "ctx")),
        P(("seq", "ctx"), None),
        P(("seq", "ctx")),
        P(("seq", "ctx")),
        P(("seq", "ctx")),
        P("seq", "ctx", None),
    )
    out_specs = (
        P("seq", "ctx", None),
        P("seq", "ctx", None),
        P(("seq", "ctx"), None),
        P(("seq", "ctx")),
        P(("seq", "ctx"), None),
        P(("seq", "ctx"), None),
        P(("seq", "ctx")),
        P(("seq", "ctx"), None),
        P(("seq", "ctx")),
        P(("seq", "ctx")),
        P(("seq", "ctx")),
        P(("seq", "ctx"), None),
        P(("seq", "ctx")),
        P(("seq", "ctx"), None),
        P(("seq", "ctx")),
        P(("seq", "ctx")),
        P(("seq", "ctx")),
    )
    return jax.shard_map(
        on_device, mesh=mesh, in_specs=in_specs, out_specs=out_specs, check_vma=False
    )
```

profile of v0, /device:TPU:0, one launch (start us, length us, event | category | flops | bytes accessed | tf_op | source)
XLA Modules:
  0.0 1621.3 jit_solution(14718962234162158246)
XLA Ops:
  19.8 42.4 %all-reduce.19 = (bf16[768]{0:T(1024)(128)(2,1)S(1)}, bf16[768]{0:T(1024)(128)(2,1)S(1)}, bf16[768]{0:T(1024)(128)(2,1)S(1)}, bf16[768]{0:T(1024)(128)(2,1)S(1)}...) all-reduce(bf16[768]{0:T(1024)(128)(2,1)S(1)} %dynamic-update-slice, ...), channel_id=1, replica_groups=mesh['seq'=4,'ctx'=8] {'seq','ctx'}, use_global_device_ids=true, to_apply=%add | all-reduce | flops 9216 | bytes 36864
  62.2 6.5 all-gather.16.cloned.1.call-done
  72.0 53.6 %all-gather.10.cloned.1.call-done = bf16[768,768]{1,0:T(8,128)(2,1)} async-done(((bf16[24,768]{1,0:T(8,128)(2,1)}), bf16[768,768]{1,0:T(8,128)(2,1)}) %all-gather.10.cloned.1.call-update) | async-done | bytes 1179664 | tf_op jit(solution)/shard_map/all_gather | solution.py:84
  131.0 12.9 all-gather
  145.7 36.7 %all-gather.14.cloned.1.call-done = bf16[768,768]{1,0:T(8,128)(2,1)} async-done(((bf16[24,768]{1,0:T(8,128)(2,1)}), bf16[768,768]{1,0:T(8,128)(2,1)}) %all-gather.14.cloned.1.call-update) | async-done | bytes 1179664 | tf_op jit(solution)/shard_map/all_gather | solution.py:82
  185.6 62.6 %all-gather.18.cloned.1.call-done = bf16[4096,768]{1,0:T(8,128)(2,1)} async-done(((bf16[512,768]{1,0:T(8,128)(2,1)}), bf16[4096,768]{1,0:T(8,128)(2,1)}) %all-gather.18.cloned.1.call-update) | async-done | bytes 6291472 | tf_op jit(solution)/shard_map/all_gather | solution.py:137
  248.2 8.6 copy.70
  256.9 56.9 %all-gather.12.cloned.1.call-done = bf16[4096,768]{1,0:T(8,128)(2,1)} async-done(((bf16[512,768]{1,0:T(8,128)(2,1)}), bf16[4096,768]{1,0:T(8,128)(2,1)}) %all-gather.12.cloned.1.call-update) | async-done | bytes 6291472 | tf_op jit(solution)/shard_map/all_gather | solution.py:136
  313.7 8.7 copy.69
  322.5 170.9 %while.34 = (s32[]{:T(128)}, f32[512,12]{0,1:T(8,128)S(1)}, f32[512,12]{0,1:T(8,128)S(1)}, f32[512,12,64]{0,2,1:T(8,128)S(1)}, s32[4096]{0:T(1024)S(1)}, /*index...) while((s32[]{:T(128)}, f32[512,12]{0,1:T(8,128)S(1)}, ...), condition=%wide.region_3.4_spmd.clone, body=%wide.region_0.3_spmd.clone.sunk | while | flops 841381888 | bytes 98181336 | solution.py:164
  324.3 7.7 fusion.125
  332.0 7.3 fusion.126
  345.4 7.7 fusion.125
  353.1 7.4 fusion.126
  366.7 7.7 fusion.125
  374.4 7.3 fusion.126
  388.0 7.7 fusion.125
  395.7 7.4 fusion.126
  409.3 8.0 fusion.125
  417.3 7.3 fusion.126
  430.8 7.7 fusion.125
  438.6 7.3 fusion.126
  452.0 7.7 fusion.125
  459.7 7.3 fusion.126
  473.3 7.7 fusion.125
  481.0 7.9 fusion.126
  497.7 21.3 %multiply_convert_fusion = (bf16[512,3072]{1,0:T(8,128)(2,1)}, f32[512,3072]{1,0:T(8,128)}, f32[512,3072]{1,0:T(8,128)}) fusion(f32[3072]{0:T(1024)S(1)} %convert_element_type.191, bf16[768,3072]{1,0:T(8,128)(2,1)} %all-gather.22.cloned.1.call-done, f32[512,768]{1,0:T(8,128)} %copy-done.13, f32[768]{0:T(1024)S(1)} %copy-done.36, ...), kind=kOutput, calls=%fused_computation.39 | convolution fusion | flops 2521694208 | bytes 22042624 | tf_op jit(solution)/shard_map/dot_general | solution.py:181
  519.0 6.1 fusion.60
  529.4 9.0 convert_reduce_fusion
  549.1 6.1 broadcast_in_dim.126
  555.2 231.7 %while.35 = (s32[]{:T(128)}, f32[512,12,64]{0,2,1:T(8,128)}, bf16[4096,1536]{0,1:T(8,128)(2,1)}, bf16[4096,768]{0,1:T(8,128)(2,1)}, s32[4096]{0:T(1024)S(1)}, /*...) while((s32[]{:T(128)}, f32[512,12,64]{0,2,1:T(8,128)}, ...), condition=%wide.region_14.15_spmd.clone, body=%wide.region_13.14_spmd.clone.sunk | while | flops 2050097152 | bytes 118047072 | solution.py:255
  561.3 5.5 fusion.139
  566.8 4.6 convolution_multiply_fusion.2
  571.3 5.0 fusion.140
  590.2 5.5 fusion.139
  595.7 4.6 convolution_multiply_fusion.2
  600.3 5.0 fusion.140
  619.1 5.5 fusion.139
  624.6 4.6 convolution_multiply_fusion.2
  629.2 5.0 fusion.140
  648.1 5.5 fusion.139
  653.6 4.6 convolution_multiply_fusion.2
  658.2 5.0 fusion.140
  677.0 5.5 fusion.139
  682.5 4.6 convolution_multiply_fusion.2
  687.1 5.0 fusion.140
  706.0 5.5 fusion.139
  711.5 4.6 convolution_multiply_fusion.2
  716.1 5.0 fusion.140
  734.9 5.5 fusion.139
  740.4 4.6 convolution_multiply_fusion.2
  745.0 5.0 fusion.140
  763.9 5.5 fusion.139
  773.9 5.0 fusion.140
  794.7 8.8 fusion.52
  804.7 8.3 fusion.64
  813.0 102.2 %reduce-scatter.14.cloned.1.call-done = bf16[512,1536]{0,1:T(8,128)(2,1)} async-done(((bf16[4096,1536]{0,1:T(8,128)(2,1)}), bf16[512,1536]{0,1:T(8,128)(2,1)}) %reduce-scatter.14.cloned.1.call-update) | async-done | bytes 1572880 | tf_op jit(solution)/shard_map/reduce_scatter | solution.py:261
  928.1 38.7 %all-reduce.18 = (f32[768]{0:T(1024)S(1)}, f32[768]{0:T(1024)S(1)}, f32[768]{0:T(1024)S(1)}, f32[768]{0:T(1024)S(1)}, f32[768]{0:T(1024)S(1)}, /*index=5*/f32[30...) all-reduce(f32[768]{0:T(1024)S(1)} %reduce_sum.219, ...), channel_id=5, replica_groups=mesh['seq'=4,'ctx'=8] {'seq','ctx'}, use_global_device_ids=true, to_apply=%region_18.19.clone | all-reduce | flops 9216 | bytes 73728
  978.0 40.2 %reduce-scatter.16.cloned.1.call-done = f32[24,768]{1,0:T(8,128)} async-done(((f32[768,768]{1,0:T(8,128)}), f32[24,768]{1,0:T(8,128)}) %reduce-scatter.16.cloned.1.call-update) | async-done | bytes 73744 | tf_op jit(solution)/shard_map/reduce_scatter | solution.py:288
  1018.2 104.8 %reduce-scatter.22.cloned.1.call-done = f32[24,768]{1,0:T(8,128)} async-done(((f32[768,768]{1,0:T(8,128)}), f32[24,768]{1,0:T(8,128)}) %reduce-scatter.22.cloned.1.call-update) | async-done | bytes 73744
  1123.0 140.8 %reduce-scatter.18.cloned.1.call-done = f32[24,3072]{1,0:T(8,128)} async-done(((f32[768,3072]{1,0:T(8,128)}), f32[24,3072]{1,0:T(8,128)}) %reduce-scatter.18.cloned.1.call-update) | async-done | bytes 294928 | tf_op jit(solution)/shard_map/reduce_scatter | solution.py:292
  1263.8 142.2 %reduce-scatter.20.cloned.1.call-done = f32[96,768]{1,0:T(8,128)} async-done(((f32[3072,768]{1,0:T(8,128)}), f32[96,768]{1,0:T(8,128)}) %reduce-scatter.20.cloned.1.call-update) | async-done | bytes 294928 | tf_op jit(solution)/shard_map/reduce_scatter | solution.py:294
  1406.0 103.9 %reduce-scatter.24.cloned.1.call-done = f32[24,768]{1,0:T(8,128)} async-done(((f32[768,768]{1,0:T(8,128)}), f32[24,768]{1,0:T(8,128)}) %reduce-scatter.24.cloned.1.call-update) | async-done | bytes 73744
  1509.9 104.6 %reduce-scatter.26.cloned.1.call-done = f32[24,768]{1,0:T(8,128)} async-done(((f32[768,768]{1,0:T(8,128)}), f32[24,768]{1,0:T(8,128)}) %reduce-scatter.26.cloned.1.call-update) | async-done | bytes 73744
  (423 shorter events, 242.7 us)
Async XLA Ops:
  7.2 118.5 %copy-start.11 = (bf16[1,512,768]{2,1,0:T(8,128)(2,1)S(1)}, bf16[1,512,768]{2,1,0:T(8,128)(2,1)}, u32[]{:S(2)}) copy-start(bf16[1,512,768]{2,1,0:T(8,128)(2,1)} %param.23) | copy-start | bytes 2359300
  7.2 61.6 %all-gather.16.cloned.1.call-start = ((), (), s32[]{:S(2)}) async-start(), calls=%async_computation.10 | async-start | bytes 1216512 | tf_op jit(solution)/shard_map/all_gather | solution.py:85
  8.8 116.8 %all-gather.10.cloned.1.call-start = ((), (), s32[]{:S(2)}) async-start(), calls=%async_computation.7 | async-start | bytes 1216512 | tf_op jit(solution)/shard_map/all_gather | solution.py:84
  10.4 172.0 %all-gather.14.cloned.1.call-start = ((), (), s32[]{:S(2)}) async-start(), calls=%async_computation.9 | async-start | bytes 1216512 | tf_op jit(solution)/shard_map/all_gather | solution.py:82
  12.0 236.2 %all-gather.18.cloned.1.call-start = ((), (), s32[]{:S(2)}) async-start(), calls=%async_computation.11 | async-start | bytes 7077888 | tf_op jit(solution)/shard_map/all_gather | solution.py:137
  71.9 56.7 %copy-start.27 = (f32[24,768]{1,0:T(8,128)S(1)}, f32[24,768]{1,0:T(8,128)}, u32[]{:S(2)}) copy-start(f32[24,768]{1,0:T(8,128)} %param.31) | copy-start | bytes 221188
  71.9 57.4 %copy-start.25 = (f32[24,3072]{1,0:T(8,128)S(1)}, f32[24,3072]{1,0:T(8,128)}, u32[]{:S(2)}) copy-start(f32[24,3072]{1,0:T(8,128)} %param.35) | copy-start | bytes 884740
  71.9 58.2 %copy-start.26 = (f32[96,768]{1,0:T(8,128)S(1)}, f32[96,768]{1,0:T(8,128)}, u32[]{:S(2)}) copy-start(f32[96,768]{1,0:T(8,128)} %param.37) | copy-start | bytes 884740
  71.9 59.0 %copy-start.42 = (s32[1,512]{1,0:T(1,128)S(1)}, s32[1,512]{1,0:T(1,128)}, u32[]{:S(2)}) copy-start(s32[1,512]{1,0:T(1,128)} %param.25) | copy-start | bytes 6148
  72.0 59.0 %copy-start.43 = (s32[1,512]{1,0:T(1,128)S(1)}, s32[1,512]{1,0:T(1,128)}, u32[]{:S(2)}) copy-start(s32[1,512]{1,0:T(1,128)} %param.24) | copy-start | bytes 6148
  72.0 241.7 %all-gather.12.cloned.1.call-start = ((), (), s32[]{:S(2)}) async-start(), calls=%async_computation.8 | async-start | bytes 7077888 | tf_op jit(solution)/shard_map/all_gather | solution.py:136
  128.6 365.0 %all-gather.20.cloned.1.call-start = ((), (), s32[]{:S(2)}) async-start(), calls=%async_computation.12 | async-start | bytes 1216512 | tf_op jit(solution)/shard_map/all_gather | solution.py:87
  129.3 368.3 %all-gather.22.cloned.1.call-start = ((), (), s32[]{:S(2)}) async-start(), calls=%async_computation.13 | async-start | bytes 4866048 | tf_op jit(solution)/shard_map/all_gather | solution.py:91
  130.1 388.9 %all-gather.24.cloned.1.call-start = ((), (), s32[]{:S(2)}) async-start(), calls=%async_computation.14 | async-start | bytes 4866048 | tf_op jit(solution)/shard_map/all_gather | solution.py:93
  130.8 784.3 %reduce-scatter.14.cloned.1.call-start = ((), (), s32[]{:S(2)}) async-start(), calls=%async_computation.15 | async-start | bytes 14155776 | tf_op jit(solution)/shard_map/reduce_scatter | solution.py:261
  322.5 171.2 %copy-start.39 = (f32[768]{0:T(1024)S(1)}, f32[768]{0:T(1024)}, u32[]{:S(2)}) copy-start(f32[768]{0:T(1024)} %convert_element_type.183) | copy-start | bytes 9220
  332.0 8.2 copy-start
  353.1 8.3 copy-start
  374.4 8.3 copy-start
  395.7 8.3 copy-start
  417.3 8.3 copy-start
  438.6 8.2 copy-start
  459.7 8.3 copy-start
  481.0 8.9 copy-start
  493.6 4.0 copy-start.16
  493.6 4.0 copy-start.36
  497.6 44.5 %copy-start.34 = (f32[512]{0:T(512)}, f32[512]{0:T(512)S(1)}, u32[]{:S(2)}) copy-start(f32[512]{0:T(512)S(1)} %fusion.50) | copy-start | bytes 6148
  497.6 21.4 %copy-start.14 = (f32[512,768]{1,0:T(8,128)S(1)}, f32[512,768]{1,0:T(8,128)}, u32[]{:S(2)}) copy-start(f32[512,768]{1,0:T(8,128)} %copy-done.13) | copy-start | bytes 4718596
  497.6 21.4 %copy-start.38 = (f32[768]{0:T(1024)S(1)}, f32[768]{0:T(1024)}, u32[]{:S(2)}) copy-start(f32[768]{0:T(1024)} %convert_element_type.195) | copy-start | bytes 9220
  519.0 6.4 copy-start.9
  525.4 3.9 slice-start.2
  528.6 9.8 slice-start
  529.4 9.0 copy-start.23
  529.4 9.0 slice-start.1
  538.4 3.7 copy-start.46
  542.1 3.5 copy-start.45
  542.7 4.9 copy-start.28
  566.8 4.6 copy-start.3
  586.6 3.3 copy-start.1
  595.7 4.6 copy-start.3
  615.6 3.3 copy-start.1
  624.6 4.6 copy-start.3
  653.6 4.6 copy-start.3
  682.5 4.6 copy-start.3
  711.5 4.6 copy-start.3
  740.4 4.6 copy-start.3
  769.4 4.6 copy-start.3
  786.9 3.6 copy-start.6
  787.0 231.3 %reduce-scatter.16.cloned.1.call-start = ((), (), s32[]{:S(2)}) async-start(), calls=%async_computation.16 | async-start | bytes 2433024 | tf_op jit(solution)/shard_map/reduce_scatter | solution.py:288
  790.5 332.5 %reduce-scatter.22.cloned.1.call-start = ((), (), s32[]{:S(2)}) async-start(), calls=%async_computation.19 | async-start | bytes 2433024
  794.4 469.4 %reduce-scatter.18.cloned.1.call-start = ((), (), s32[]{:S(2)}) async-start(), calls=%async_computation.17 | async-start | bytes 9732096 | tf_op jit(solution)/shard_map/reduce_scatter | solution.py:292
  803.6 602.4 %reduce-scatter.20.cloned.1.call-start = ((), (), s32[]{:S(2)}) async-start(), calls=%async_computation.18 | async-start | bytes 9732096 | tf_op jit(solution)/shard_map/reduce_scatter | solution.py:294
  813.0 697.0 %reduce-scatter.24.cloned.1.call-start = ((), (), s32[]{:S(2)}) async-start(), calls=%async_computation.20 | async-start | bytes 2433024
  919.1 695.4 %reduce-scatter.26.cloned.1.call-start = ((), (), s32[]{:S(2)}) async-start(), calls=%async_computation.21 | async-start | bytes 2433024
  923.1 4.9 copy-start.30
  923.1 4.9 copy-start.31
  923.1 4.9 copy-start.32
  923.1 4.9 copy-start.33
  923.1 4.9 copy-start.40
  923.1 4.9 copy-start.41
  926.5 47.8 %copy-start.8 = (f32[512,768]{1,0:T(8,128)S(1)}, f32[512,768]{1,0:T(8,128)}, u32[]{:S(2)}) copy-start(f32[512,768]{1,0:T(8,128)} %copy-done.7) | copy-start | bytes 4718596
  926.5 47.9 %copy-start.15 = (bf16[512,1536]{0,1:T(8,128)(2,1)S(1)}, bf16[512,1536]{0,1:T(8,128)(2,1)}, u32[]{:S(2)}) copy-start(bf16[512,1536]{0,1:T(8,128)(2,1)} %reduce-scatter.14.cloned.1.call-done) | copy-start | bytes 4718596
  926.5 47.9 %copy-start.29 = (f32[512]{0:T(512)S(1)}, f32[512]{0:T(512)}, u32[]{:S(2)}) copy-start(f32[512]{0:T(512)} %copy-done.28) | copy-start | bytes 6148
  966.8 7.6 copy-start.22
  (44 other events, 95.5 us)
Sparse Core Ops, SparseCore 0:
  11.6 57.0 all-gather.15
  72.4 53.2 all-gather.9
  129.3 53.1 all-gather.13
  184.5 63.6 all-gather.17
  250.3 63.3 all-gather.11
  317.2 52.8 all-gather.19
  373.6 62.6 all-gather.21
  439.9 62.4 all-gather.23
  787.1 128.0 reduce-scatter.13
  920.9 97.2 reduce-scatter.15
  1025.0 97.9 reduce-scatter.21
  1129.3 134.4 reduce-scatter.17
  1271.3 134.6 reduce-scatter.19
  1411.7 98.1 reduce-scatter.23
  1516.5 97.9 reduce-scatter.25
where the time goes:
time: 1630 us; the launch traced here: 1620 us
  waiting for transfers between devices  955 us (59%)
  matrix products  350 us (21%)
  other arithmetic  109 us (7%)
  local copies, waits for them, and re-layouts  95.5 us (6%)
  blocking collectives  94 us (6%)
    unnamed x18, waiting for transfers between devices  314 us
    reduce_scatter x1, waiting for transfers between devices, on_device(): lax.psum_scatter(grad_proj_down, ('seq', 'ctx'), scatter_dimension=0, til...  142 us
    reduce_scatter x1, waiting for transfers between devices, on_device(): lax.psum_scatter(grad_proj_up, ('seq', 'ctx'), scatter_dimension=0, tiled...  141 us
    reduce_scatter x1, waiting for transfers between devices, on_device(): lax.psum_scatter(grad_pairs.astype(jnp.bfloat16), 'ctx', scatter_dimensio...  102 us
    dot_general x16, matrix products, score_block(): jnp.einsum('qhd,khd->qhk', query_heads, key_heads, preferred_element_type...  87.9 us
    unnamed x2, blocking collectives  81.1 us
    all_gather x1, waiting for transfers between devices, on_device(): value_piece = lax.all_gather(values, 'ctx', axis=0, tiled=True)  62.6 us
    reduce_sum x8, other arithmetic, attend_inner(): running_sum = running_sum * fading + jnp.sum(probability, axis=-1)  59.3 us
  transfers between devices with their start and end apart: 15, of which 12 were waited for; matrix products, arithmetic and copies ran while one was open for 17% of the time, Pallas kernels for 0%

commit v1 on v0

v1 whole, which is shorter than its diff:
```python
import math
from functools import partial

import jax
import jax.numpy as jnp
from jax import lax
from jax.experimental import pallas as pl
from jax.experimental.pallas import tpu as pltpu
from jax.sharding import PartitionSpec as P

H = 12
DH = 64
VMEM_LIMIT = 60 * 1024 * 1024

LOG2E = 1.4426950408889634
BQ = 512
BK = 512
HALF = BK // 2
PAD = BK + HALF
LANES = 128


def nt(a, b):
    return lax.dot_general(a, b, (((1,), (1,)), ((), ())), preferred_element_type=jnp.float32)


def nn(a, b):
    return lax.dot_general(a, b, (((1,), (0,)), ((), ())), preferred_element_type=jnp.float32)


def code_columns(seg_ref, val_ref, kcode, pad):
    count, width = seg_ref.shape
    for i in range(count):
        code = (seg_ref[i : i + 1, :] * 2 + val_ref[i : i + 1, :]).astype(jnp.float32)
        for j in range(width // LANES):
            piece = code[:, j * LANES : (j + 1) * LANES]
            at = i * width + j * LANES
            kcode[at : at + LANES, :] = jnp.broadcast_to(piece, (LANES, LANES)).T
    kcode[count * width :, :] = jnp.full((pad, LANES), -1.0, jnp.float32)


def total(values):
    return jnp.sum(values.astype(jnp.float32)).astype(jnp.int32)


def key_range(seg_ref, val_ref, block, start):
    seg = seg_ref[...]
    val = val_ref[...]
    count, width = seg.shape
    position = lax.broadcasted_iota(jnp.int32, (count, width), 0) * width + lax.broadcasted_iota(
        jnp.int32, (count, width), 1
    )
    in_block = (position >= start) & (position < start + block)
    low = jnp.min(jnp.where(in_block, seg, 1 << 20).astype(jnp.float32)).astype(jnp.int32)
    high = jnp.max(jnp.where(in_block, seg, -1).astype(jnp.float32)).astype(jnp.int32)
    length = count * width
    first = total(seg < low)
    end = total(seg <= high)
    last_valid = jnp.max(jnp.where(val == 1, position + 1, 0).astype(jnp.float32)).astype(jnp.int32)
    first_invalid = jnp.min(jnp.where(val == 1, length, position).astype(jnp.float32)).astype(jnp.int32)
    end = jnp.minimum(end, last_valid)
    origin = first // LANES * LANES
    blocks = (end - origin + BK - 1) // BK
    clear_end = jnp.minimum(end, first_invalid)
    clear_from = (first - origin + BK - 1) // BK
    clear_to = jnp.maximum(clear_end - origin, 0) // BK
    one_document = low == high
    clear_from = jnp.where(one_document, jnp.minimum(clear_from, blocks), blocks)
    clear_to = jnp.where(one_document, jnp.minimum(jnp.maximum(clear_to, clear_from), blocks), blocks)
    return origin, blocks, clear_from, clear_to


def attend_kernel(
    heads, chunks, ctx_axis, repeat,
    x_ref, w_ref, bias_ref, seg_ref, val_ref,
    k_out, v_out, q_out, of_out, ob_out, lse_out,
    kcode, q_ext, k_ext, v_ext, s_even, s_odd,
):
    width = heads * DH
    length = x_ref.shape[0]
    rows = length // (chunks * repeat)
    place = lax.rem(lax.axis_index(ctx_axis), repeat)
    code_columns(seg_ref, val_ref, kcode, PAD)
    wt = w_ref[...].astype(jnp.float32).T.astype(jnp.bfloat16)
    wq, wv = wt[:width], wt[2 * width : 3 * width]
    bias_q = bias_ref[0:width, 0:1]
    bias_v = bias_ref[width : 2 * width, 0:1]

    def keys(i, carry):
        at = pl.multiple_of(i * rows, LANES)
        x = x_ref[pl.ds(at, rows), :]
        k = nn(x, w_ref[:, width : 2 * width]).astype(jnp.bfloat16)
        v = (nt(wv, x) + bias_v).astype(jnp.bfloat16)
        v_out[:, pl.ds(at, rows)] = v
        for h in range(heads):
            one = k[:, h * DH : (h + 1) * DH]
            k_out[h, pl.ds(at, rows), :] = one
            k_ext[h, pl.ds(at, rows), :] = jnp.concatenate([one, one], axis=1)
            v_ext[h, 0:DH, pl.ds(at, rows)] = v[h * DH : (h + 1) * DH]
        return carry

    lax.fori_loop(0, chunks * repeat, keys, 0)
    k_out[:, length:, :] = jnp.zeros((heads, PAD, DH), jnp.bfloat16)
    k_ext[:, length:, :] = jnp.zeros((heads, PAD, 2 * DH), jnp.bfloat16)
    v_ext[:, 0:DH, length:] = jnp.zeros((heads, DH, PAD), jnp.bfloat16)
    v_ext[:, DH:, :] = jnp.ones((heads, 16, length + PAD), jnp.bfloat16)

    def queries(i, carry):
        at = pl.multiple_of((i * repeat + place) * rows, LANES)
        to = pl.ds(pl.multiple_of(i * rows, LANES), rows)
        q = (nt(wq, x_ref[pl.ds(at, rows), :]) + bias_q).astype(jnp.bfloat16)
        q_out[:, to] = q
        scaled = q.astype(jnp.float32) * (DH**-0.5 * LOG2E)
        high = scaled.astype(jnp.bfloat16)
        rest = (scaled - high.astype(jnp.float32)).astype(jnp.bfloat16)
        for h in range(heads):
            q_ext[h, 0:DH, to] = high[h * DH : (h + 1) * DH]
            q_ext[h, DH:, to] = rest[h * DH : (h + 1) * DH]
        return carry

    lax.fori_loop(0, chunks, queries, 0)
    per_chunk = rows // BQ

    def block(i, carry):
        chunk = i // per_chunk
        inner = pl.multiple_of((i - chunk * per_chunk) * BQ, LANES)
        start = (chunk * repeat + place) * rows + inner
        origin, blocks, clear_from, clear_to = key_range(seg_ref, val_ref, BQ, start)
        at = pl.multiple_of(i * BQ, LANES)
        which = chunk * repeat + place
        target = (seg_ref[pl.ds(which, 1), pl.ds(inner, BQ)] * 2 + 1).astype(jnp.float32)

        def scores(slot, key_at):
            for h in range(heads):
                slot[h] = nn(k_ext[h, pl.ds(key_at, HALF), :], q_ext[h, :, pl.ds(at, BQ)])

        def soften(masked, slot, key_at, state):
            if masked:
                code = kcode[pl.ds(key_at, HALF), :]
                allowed = jnp.concatenate([code] * (BQ // LANES), axis=1) == target
            fresh = []
            for h in range(heads):
                top, acc = state[2 * h : 2 * h + 2]
                s = slot[h]
                if masked:
                    s = jnp.where(allowed, s, -1e30)
                new = jnp.maximum(top, jnp.max(s, axis=0, keepdims=True))
                p = jnp.exp2(s - new).astype(jnp.bfloat16)
                acc = acc * jnp.exp2(top - new) + nn(v_ext[h, :, pl.ds(key_at, HALF)], p)
                fresh += [new, acc]
            return tuple(fresh)

        def step(masked, j, state):
            first = pl.multiple_of(origin + j * BK, LANES)
            second = pl.multiple_of(first + HALF, LANES)
            scores(s_odd, second)
            state = soften(masked, s_even, first, state)
            scores(s_even, pl.multiple_of(first + BK, LANES))
            return soften(masked, s_odd, second, state)

        state = ()
        for h in range(heads):
            state += (jnp.full((1, BQ), -1e30, jnp.float32), jnp.zeros((DH + 16, BQ), jnp.float32))
        scores(s_even, pl.multiple_of(origin, LANES))
        state = lax.fori_loop(0, clear_from, partial(step, True), state)
        state = lax.fori_loop(clear_from, clear_to, partial(step, False), state)
        state = lax.fori_loop(clear_to, blocks, partial(step, True), state)
        for h in range(heads):
            top, acc = state[2 * h : 2 * h + 2]
            low = acc[DH : DH + 1]
            out = acc[0:DH] / low
            of_out[h * DH : (h + 1) * DH, pl.ds(at, BQ)] = out
            ob_out[chunk, h * DH : (h + 1) * DH, pl.ds(inner, BQ)] = out.astype(jnp.bfloat16)
            lse_out[h : h + 1, pl.ds(at, BQ)] = top + jnp.log2(low)
        return carry

    lax.fori_loop(0, chunks * per_chunk, block, 0)


def attend(x, w, bias, seg, val, heads, chunks):
    length = x.shape[0]
    width = heads * DH
    count, rows = seg.shape
    repeat = count // chunks
    mine = chunks * rows
    shape = jax.ShapeDtypeStruct
    whole = pl.BlockSpec(memory_space=pltpu.VMEM)
    return pl.pallas_call(
        partial(attend_kernel, heads, chunks, "ctx", repeat),
        out_shape=(
            shape((heads, length + PAD, DH), jnp.bfloat16),
            shape((width, length), jnp.bfloat16),
            shape((width, mine), jnp.bfloat16),
            shape((width, mine), jnp.float32),
            shape((chunks, width, rows), jnp.bfloat16),
            shape((8, mine), jnp.float32),
        ),
        in_specs=[whole] * 5,
        out_specs=(whole,) * 6,
        scratch_shapes=[
            pltpu.VMEM((length + PAD, LANES), jnp.float32),
            pltpu.VMEM((heads, 2 * DH, mine), jnp.bfloat16),
            pltpu.VMEM((heads, length + PAD, 2 * DH), jnp.bfloat16),
            pltpu.VMEM((heads, DH + 16, length + PAD), jnp.bfloat16),
            pltpu.VMEM((heads, HALF, BQ), jnp.float32),
            pltpu.VMEM((heads, HALF, BQ), jnp.float32),
        ],
        compiler_params=pltpu.CompilerParams(vmem_limit_bytes=VMEM_LIMIT),
        name="attend",
    )(x, w, bias, seg, val)


def tn(a, b):
    return lax.dot_general(a, b, (((0,), (0,)), ((), ())), preferred_element_type=jnp.float32)


def flip(a):
    return a.astype(jnp.float32).T.astype(a.dtype)


def three_parts(row):
    high = row.astype(jnp.bfloat16)
    rest = row - high.astype(jnp.float32)
    middle = rest.astype(jnp.bfloat16)
    low = (rest - middle.astype(jnp.float32)).astype(jnp.bfloat16)
    empty = jnp.zeros((13, row.shape[1]), jnp.float32)
    return jnp.concatenate(
        [high.astype(jnp.float32), middle.astype(jnp.float32), low.astype(jnp.float32), empty], axis=0
    )


def retreat_kernel(
    heads, chunks, ctx_axis, repeat,
    x_ref, w_ref, k_ref, v_ref, q_ref, o_ref, lse_ref, do_ref, seg_ref, val_ref,
    dx_out, dw_out, db_out,
    krow, target, q_ext, kt_ext, v_ext, do_ext, do_rows, dq, dkv,
    s_even, s_odd, g_even, g_odd, dw, x_slot, dx_slot, in_sem, out_sem, v_sem,
):
    width = heads * DH
    length = x_ref.shape[0]
    count = chunks * repeat
    rows = length // (chunks * repeat)
    mine = chunks * rows
    place = lax.rem(lax.axis_index(ctx_axis), repeat)
    bf16 = jnp.bfloat16

    def fetch(i):
        slot = lax.rem(i, 2)
        source = x_ref.at[pl.ds(pl.multiple_of(i * rows, LANES), rows)]
        return pltpu.make_async_copy(source, x_slot.at[slot], in_sem.at[slot])

    def deliver(i):
        slot = lax.rem(i, 2)
        return pltpu.make_async_copy(dx_slot.at[slot], dx_out.at[i], out_sem.at[slot])

    fetch(0).start()
    values = [
        pltpu.make_async_copy(
            v_ref.at[pl.ds(h * DH, DH)], v_ext.at[h, pl.ds(0, DH), pl.ds(0, length)], v_sem.at[h]
        )
        for h in range(heads)
    ]
    for copy in values:
        copy.start()
    for i in range(chunks * repeat):
        code = (seg_ref[i : i + 1, :] * 2 + val_ref[i : i + 1, :]).astype(jnp.float32)
        krow[:, i * rows : (i + 1) * rows] = jnp.broadcast_to(code, (8, rows))
    krow[:, length:] = jnp.full((8, PAD), -1.0, jnp.float32)

    def keys(i, carry):
        at = pl.ds(pl.multiple_of(i * rows, LANES), rows)
        for h in range(heads):
            kt = flip(k_ref[h, at, :])
            kt_ext[h, 0:DH, at] = kt
            kt_ext[h, DH : 2 * DH, at] = kt
        return carry

    lax.fori_loop(0, chunks * repeat, keys, 0)
    kt_ext[:, 0 : 2 * DH, length:] = jnp.zeros((heads, 2 * DH, PAD), bf16)
    v_ext[:, 0:DH, length:] = jnp.zeros((heads, DH, PAD), bf16)
    kt_ext[:, 2 * DH :, :] = jnp.ones((heads, 16, length + PAD), bf16)
    v_ext[:, DH:, :] = jnp.ones((heads, 16, length + PAD), bf16)
    dkv[...] = jnp.zeros(dkv.shape, jnp.float32)
    dq[...] = jnp.zeros(dq.shape, jnp.float32)

    def queries(i, carry):
        at = pl.ds(pl.multiple_of(i * rows, LANES), rows)
        which = i * repeat + place
        code = (seg_ref[pl.ds(which, 1), :] * 2 + 1).astype(jnp.float32)
        for j in range(rows // LANES):
            piece = code[:, j * LANES : (j + 1) * LANES]
            target[pl.ds(pl.multiple_of(i * rows + j * LANES, LANES), LANES), :] = jnp.broadcast_to(
                piece, (LANES, LANES)
            ).T
        for h in range(heads):
            part = slice(h * DH, (h + 1) * DH)
            scaled = q_ref[part, at].astype(jnp.float32) * (DH**-0.5 * LOG2E)
            high = scaled.astype(bf16).astype(jnp.float32)
            extra = three_parts(-lse_ref[h : h + 1, at])
            full = jnp.concatenate([high, scaled - high, extra], axis=0)
            q_ext[h, at, :] = full.T.astype(bf16)
            grad = do_ref[i, part, :].astype(jnp.float32)
            delta = jnp.sum(grad * o_ref[part, at], axis=0, keepdims=True)
            do_rows[part, at] = do_ref[i, part, :]
            do_ext[h, at, :] = jnp.concatenate([grad, three_parts(-delta)], axis=0).T.astype(bf16)
        return carry

    lax.fori_loop(0, chunks, queries, 0)
    per_chunk = rows // BQ

    def block(i, carry):
        chunk = i // per_chunk
        inner = (i - chunk * per_chunk) * BQ
        start = (chunk * repeat + place) * rows + inner
        origin, blocks, clear_from, clear_to = key_range(seg_ref, val_ref, BQ, start)
        at = pl.ds(pl.multiple_of(i * BQ, LANES), BQ)

        def scores(s_slot, g_slot, key_at):
            key = pl.ds(key_at, HALF)
            for h in range(heads):
                s_slot[h] = nn(q_ext[h, at, :], kt_ext[h, :, key])
                g_slot[h] = nn(do_ext[h, at, :], v_ext[h, :, key])

        def absorb(masked, s_slot, g_slot, key_at):
            key = pl.ds(key_at, HALF)
            if masked:
                code = krow[0:1, key]
                wanted = jnp.concatenate([target[at, :]] * (HALF // LANES), axis=1)
                allowed = wanted == code
            for h in range(heads):
                part = slice(h * DH, (h + 1) * DH)
                p = jnp.exp2(s_slot[h])
                if masked:
                    p = jnp.where(allowed, p, 0.0)
                ds = (p * g_slot[h]).astype(bf16)
                dkv[width + h * DH : width + (h + 1) * DH, key] += nn(do_rows[part, at], p.astype(bf16))
                dkv[part, key] += nn(q_ref[part, at], ds)
                dq[h, at, :] += nn(ds, k_ref[h, key, :])

        def step(masked, j, carry):
            first = pl.multiple_of(origin + j * BK, LANES)
            second = pl.multiple_of(first + HALF, LANES)
            scores(s_odd, g_odd, second)
            absorb(masked, s_even, g_even, first)
            scores(s_even, g_even, pl.multiple_of(first + BK, LANES))
            absorb(masked, s_odd, g_odd, second)
            return carry

        scores(s_even, g_even, pl.multiple_of(origin, LANES))
        lax.fori_loop(0, clear_from, partial(step, True), 0)
        lax.fori_loop(clear_from, clear_to, partial(step, False), 0)
        lax.fori_loop(clear_to, blocks, partial(step, True), 0)
        return carry

    for copy in values:
        copy.wait()
    lax.fori_loop(0, chunks * per_chunk, block, 0)

    wt = w_ref[...].astype(jnp.float32).T.astype(bf16)
    scale = DH**-0.5
    one = jnp.ones((8, rows), bf16)
    dw[...] = jnp.zeros(dw.shape, jnp.float32)
    db_out[...] = jnp.zeros(db_out.shape, jnp.float32)

    def spread(i, carry):
        slot = lax.rem(i, 2)

        @pl.when(i + 1 < count)
        def _():
            fetch(i + 1).start()

        fetch(i).wait()

        @pl.when(i >= 2)
        def _():
            deliver(i - 2).wait()

        at = pl.ds(pl.multiple_of(i * rows, LANES), rows)
        dk = (dkv[0:width, at] * scale).astype(bf16)
        dv = dkv[width:, at].astype(bf16)
        both = jnp.concatenate([dk, dv], axis=0)
        dx_slot[slot] = tn(both, wt[width : 3 * width]).astype(bf16)
        dw[width : 3 * width, :] += nn(both, x_slot[slot])
        db_out[:, width:] += nt(one, dv)

        @pl.when(lax.rem(i, repeat) == place)
        def _():
            own = pl.ds(pl.multiple_of(i // repeat * rows, LANES), rows)
            grad = jnp.concatenate([dq[h, own, :] for h in range(heads)], axis=1) * scale
            grad = grad.astype(bf16)
            dx_slot[slot] = (dx_slot[slot].astype(jnp.float32) + nn(grad, wt[0:width])).astype(bf16)
            dw[0:width, :] += tn(grad, x_slot[slot])
            db_out[:, 0:width] += nn(one, grad)

        deliver(i).start()
        return carry

    lax.fori_loop(0, count, spread, 0)
    deliver(count - 2).wait()
    deliver(count - 1).wait()
    dw_out[...] = dw[...].T.astype(bf16)


def retreat(x, w, k, v, q, o, lse, do, seg, val, heads, chunks):
    length, model = x.shape
    width = heads * DH
    count, rows = seg.shape
    repeat = count // chunks
    mine = chunks * rows
    shape = jax.ShapeDtypeStruct
    whole = pl.BlockSpec(memory_space=pltpu.VMEM)
    f32, bf16 = jnp.float32, jnp.bfloat16
    return pl.pallas_call(
        partial(retreat_kernel, heads, chunks, "ctx", repeat),
        out_shape=(
            shape((count, rows, model), bf16),
            shape((model, w.shape[1]), bf16),
            shape((8, 2 * width), f32),
        ),
        in_specs=[whole if i not in (0, 3) else pl.BlockSpec(memory_space=pl.ANY) for i in range(10)],
        out_specs=(pl.BlockSpec(memory_space=pl.ANY), whole, whole),
        scratch_shapes=[
            pltpu.VMEM((8, length + PAD), f32),
            pltpu.VMEM((mine, LANES), f32),
            pltpu.VMEM((heads, mine, 2 * DH + 16), bf16),
            pltpu.VMEM((heads, 2 * DH + 16, length + PAD), bf16),
            pltpu.VMEM((heads, DH + 16, length + PAD), bf16),
            pltpu.VMEM((heads, mine, DH + 16), bf16),
            pltpu.VMEM((width, mine), bf16),
            pltpu.VMEM((heads, mine, DH), f32),
            pltpu.VMEM((2 * width, length + PAD), f32),
        ]
        + [pltpu.VMEM((heads, BQ, HALF), f32)] * 4
        + [
            pltpu.VMEM((w.shape[1], model), f32),
            pltpu.VMEM((2, rows, model), bf16),
            pltpu.VMEM((2, rows, model), bf16),
            pltpu.SemaphoreType.DMA((2,)),
            pltpu.SemaphoreType.DMA((2,)),
            pltpu.SemaphoreType.DMA((heads,)),
        ],
        compiler_params=pltpu.CompilerParams(vmem_limit_bytes=VMEM_LIMIT),
        name="retreat",
    )(x, w, k, v, q, o, lse, do, seg, val)


EPSILON = 1e-12
FF_BLOCK = 512


def gelu_pair(u):
    z = jnp.abs(u) * (0.5**0.5)
    t = 1.0 / (1.0 + 0.3275911 * z)
    bell = jnp.exp(-z * z)
    poly = t * (
        0.254829592 + t * (-0.284496736 + t * (1.421413741 + t * (-1.453152027 + t * 1.061405429)))
    )
    half = 0.5 * poly * bell
    below = jnp.where(u < 0.0, half, 1.0 - half)
    return u * below, below + u * bell * 0.3989422804014327


def standard(hidden):
    centred = hidden - jnp.mean(hidden, axis=-1, keepdims=True)
    scale = lax.rsqrt(jnp.mean(centred * centred, axis=-1, keepdims=True) + EPSILON)
    return centred * scale, scale


def norm_back(grad, gain, normal, scale):
    t = grad * gain
    return scale * (
        t
        - jnp.mean(t, axis=-1, keepdims=True)
        - normal * jnp.mean(t * normal, axis=-1, keepdims=True)
    )


def middle_kernel(
    o_ref, x_ref, cot_ref, wo_ref, w1_ref, w2_ref, small_ref, b1_ref,
    out_ref, e1_ref, do_ref, dwo_ref, dw1_ref, dw2_ref, dsmall_ref, db1_ref,
    act, slope, y1_ref, normal_ref, r2_ref, y1t_ref, grad_ref,
):
    bf16 = jnp.bfloat16
    groups, width, rows = o_ref.shape
    hidden_width = w1_ref.shape[1]
    steps = hidden_width // FF_BLOCK
    row = lambda i: small_ref[i : i + 1, :]
    ones = jnp.ones((8, rows), bf16)
    o = o_ref[...].reshape(groups * width, rows)
    n1 = x_ref[...].astype(jnp.float32) + (tn(o, wo_ref[...]) + row(0))
    normal, scale_one = standard(n1)
    normal_ref[...] = normal
    y1 = normal * row(1) + row(2)
    y1_ref[...] = y1
    y1_low = y1.astype(bf16)
    y1t_ref[...] = y1.T.astype(bf16)
    grad_ref[...] = jnp.zeros(grad_ref.shape, jnp.float32)

    def forward(i, carry):
        at = pl.ds(pl.multiple_of(i * FF_BLOCK, FF_BLOCK), FF_BLOCK)
        u = nn(y1_low, w1_ref[:, at]) + b1_ref[0:1, at]
        value, gradient = gelu_pair(u)
        value = value.astype(bf16)
        act[:, at] = value
        slope[:, at] = gradient
        grad_ref[...] += nn(value, w2_ref[at, :])
        return carry

    lax.fori_loop(0, steps, forward, 0)
    normal_two, scale_two = standard(y1_ref[...] + (grad_ref[...] + row(3)))
    out_ref[...] = normal_two * row(4) + row(5)
    cot = cot_ref[...].astype(jnp.float32)
    dsmall_ref[4:5, :] = jnp.sum(cot * normal_two, axis=0, keepdims=True)
    dsmall_ref[5:6, :] = jnp.sum(cot, axis=0, keepdims=True)
    e2 = norm_back(cot, row(4), normal_two, scale_two)
    grad_ref[...] = e2
    r2 = e2.astype(bf16)
    r2_ref[...] = r2
    dsmall_ref[3:4, :] = nn(ones, r2)[0:1]

    def backward(i, carry):
        at = pl.ds(pl.multiple_of(i * FF_BLOCK, FF_BLOCK), FF_BLOCK)
        dw2_ref[at, :] = tn(act[:, at], r2_ref[...]).astype(bf16)
        du = (nt(r2_ref[...], w2_ref[at, :]) * slope[:, at]).astype(bf16)
        db1_ref[:, at] = nn(ones, du)
        dw1_ref[:, at] = nn(y1t_ref[...], du).astype(bf16)
        grad_ref[...] += nt(du, w1_ref[:, at])
        return carry

    lax.fori_loop(0, steps, backward, 0)
    grad = grad_ref[...]
    normal = normal_ref[...]
    dsmall_ref[1:2, :] = jnp.sum(grad * normal, axis=0, keepdims=True)
    dsmall_ref[2:3, :] = jnp.sum(grad, axis=0, keepdims=True)
    e1 = norm_back(grad, row(1), normal, scale_one)
    e1_ref[...] = e1
    r1 = e1.astype(bf16)
    dsmall_ref[0:1, :] = nn(ones, r1)[0:1]
    dsmall_ref[6:8, :] = jnp.zeros((2, dsmall_ref.shape[1]), jnp.float32)
    dwo_ref[...] = nn(o, r1).astype(bf16)
    do_ref[...] = nt(wo_ref[...], r1).astype(bf16).reshape(groups, width, rows)


def middle(o, x, cot, wo, w1, w2, small, b1):
    groups, width, rows = o.shape
    model = x.shape[1]
    hidden_width = w1.shape[1]
    shape = jax.ShapeDtypeStruct
    whole = pl.BlockSpec(memory_space=pltpu.VMEM)
    f32, bf16 = jnp.float32, jnp.bfloat16
    return pl.pallas_call(
        middle_kernel,
        out_shape=(
            shape((rows, model), f32),
            shape((rows, model), f32),
            shape(o.shape, bf16),
            shape(wo.shape, bf16),
            shape(w1.shape, bf16),
            shape(w2.shape, bf16),
            shape((8, model), f32),
            shape((8, hidden_width), f32),
        ),
        in_specs=[whole] * 8,
        out_specs=(whole,) * 8,
        scratch_shapes=[
            pltpu.VMEM((rows, hidden_width), bf16),
            pltpu.VMEM((rows, hidden_width), f32),
            pltpu.VMEM((rows, model), f32),
            pltpu.VMEM((rows, model), f32),
            pltpu.VMEM((rows, model), bf16),
            pltpu.VMEM((model, rows), bf16),
            pltpu.VMEM((rows, model), f32),
        ],
        compiler_params=pltpu.CompilerParams(vmem_limit_bytes=VMEM_LIMIT),
        name="middle",
    )(o, x, cot, wo, w1, w2, small, b1)


def on_device(
    tokens, segment_ids, valid_tokens, query_weight, query_bias, key_weight, value_weight, value_bias,
    output_weight, output_bias, attn_norm_gain, attn_norm_shift, up_weight, up_bias, down_weight,
    down_bias, ffn_norm_gain, ffn_norm_shift, out_cotangent,
):
    both = ("seq", "ctx")
    bf16 = jnp.bfloat16
    count = lax.axis_size("ctx")
    chunks = math.gcd(H, count)
    repeat = count // chunks
    heads = H // chunks
    width = heads * DH
    x = tokens[0]
    rows, model = x.shape
    group = lax.axis_index("ctx") // repeat

    def gather(a):
        return lax.all_gather(a.astype(bf16), both, axis=0, tiled=True)

    def share(a):
        return lax.dynamic_slice_in_dim(a, group * width, width, a.ndim - 1)

    wq, wk, wv = gather(query_weight), gather(key_weight), gather(value_weight)
    wo, w1, w2 = gather(output_weight), gather(up_weight), gather(down_weight)
    small_parts = (output_bias, attn_norm_gain, attn_norm_shift, down_bias, ffn_norm_gain, ffn_norm_shift)
    small = [gather(a).astype(jnp.float32) for a in small_parts]
    small = jnp.stack(small + [jnp.zeros_like(small[0])] * 2)
    b1 = jnp.broadcast_to(gather(up_bias).astype(jnp.float32)[None], (8, up_bias.shape[0] * lax.axis_size(both)))
    bias = jnp.concatenate([share(gather(query_bias)), share(gather(value_bias))]).astype(jnp.float32)
    bias = jnp.broadcast_to(bias[:, None], (2 * width, LANES))
    padded = -(-3 * width // LANES) * LANES
    w = jnp.concatenate(
        [share(wq), share(wk), share(wv), jnp.zeros((model, padded - 3 * width), bf16)], axis=1
    )
    x_all = lax.all_gather(x, "ctx", axis=0, tiled=True)
    seg = lax.all_gather(segment_ids[0], "ctx", axis=0)
    val = lax.all_gather(valid_tokens[0], "ctx", axis=0)
    k, v, q, o_float, o_send, lse = attend(x_all, w, bias, seg, val, heads, chunks)
    groups = [[g * repeat + r for g in range(chunks)] for r in range(repeat)]

    def exchange(a):
        return lax.all_to_all(a, "ctx", 0, 0, axis_index_groups=groups, tiled=True)

    output, e1, do, dwo, dw1, dw2, dsmall, db1 = middle(
        exchange(o_send), x, out_cotangent[0], wo, w1, w2, small, b1
    )
    dx, dw, db = retreat(x_all, w, k, v, q, o_float, lse, exchange(do), seg, val, heads, chunks)
    dx = lax.psum_scatter(dx, "ctx", scatter_dimension=0, tiled=True)[0]

    def place(a, wide):
        return lax.dynamic_update_slice_in_dim(
            jnp.zeros(a.shape[:-1] + (wide,), a.dtype), a, group * width, a.ndim - 1
        )

    def scatter(a):
        return lax.psum_scatter(a, both, scatter_dimension=0, tiled=True).astype(jnp.float32)

    dwq, dwk, dwv = [scatter(place(dw[:, i * width : (i + 1) * width], model)) for i in range(3)]
    dbq, dbv = [scatter(place(db[0, i * width : (i + 1) * width], model)) for i in range(2)]
    dbo, dg1, dc1, db2, dg2, dc2 = [scatter(dsmall[i]) for i in range(6)]
    return (
        output[None],
        (e1 + dx.astype(jnp.float32))[None],
        dwq, dbq, dwk, dwv, dbv,
        scatter(dwo), dbo, dg1, dc1,
        scatter(dw1), scatter(db1[0]), scatter(dw2), db2, dg2, dc2,
    )


def solution(mesh):
    in_specs = (
        P("seq", "ctx", None),
        P("seq", "ctx"),
        P("seq", "ctx"),
        P(("seq", "ctx"), None),
        P(("seq", "ctx")),
        P(("seq", "ctx"), None),
        P(("seq", "ctx"), None),
        P(("seq", "ctx")),
        P(("seq", "ctx"), None),
        P(("seq", "ctx")),
        P(("seq", "ctx")),
        P(("seq", "ctx")),
        P(("seq", "ctx"), None),
        P(("seq", "ctx")),
        P(("seq", "ctx"), None),
        P(("seq", "ctx")),
        P(("seq", "ctx")),
        P(("seq", "ctx")),
        P("seq", "ctx", None),
    )
    out_specs = (
        P("seq", "ctx", None),
        P("seq", "ctx", None),
        P(("seq", "ctx"), None),
        P(("seq", "ctx")),
        P(("seq", "ctx"), None),
        P(("seq", "ctx"), None),
        P(("seq", "ctx")),
        P(("seq", "ctx"), None),
        P(("seq", "ctx")),
        P(("seq", "ctx")),
        P(("seq", "ctx")),
        P(("seq", "ctx"), None),
        P(("seq", "ctx")),
        P(("seq", "ctx"), None),
        P(("seq", "ctx")),
        P(("seq", "ctx")),
        P(("seq", "ctx")),
    )
    return jax.shard_map(
        on_device, mesh=mesh, in_specs=in_specs, out_specs=out_specs, check_vma=False
    )
```

time: 1630 us -> 1190 us (0.73)
  matrix products: 350 us -> 0 us
  Pallas kernels: 0 us -> 173 us
  waiting for transfers between devices: 955 us -> 811 us
  other arithmetic: 109 us -> 20.3 us
  local copies, waits for them, and re-layouts: 95.5 us -> 34.5 us
  blocking collectives: 94 us -> 134 us
    dot_general x74 -> x0, matrix products: 350 us -> none  [the longest x16 87.9 us: score_block(): jnp.einsum('qhd,khd->qhk', query_heads, key_heads, preferred_element_type...]
    unnamed x18 -> x14, waiting for transfers between devices: 314 us -> 2.41 us
    pallas_call x0 -> x3, Pallas kernels: none -> 173 us  [the longest x1 86.3 us: retreat(): pl.pallas_call(partial(retreat_kernel, heads, chunks, 'ctx', repeat), out...]
    reduce_scatter x4 -> x7, waiting for transfers between devices: 425 us -> 519 us  [the longest x6 450 us: scatter(): lax.psum_scatter(a, both, scatter_dimension=0, tiled=True)]
    all_gather x8 -> x7, waiting for transfers between devices: 216 us -> 289 us  [the longest x6 226 us: gather(): return lax.all_gather(a.astype(bf16), both, axis=0, tiled=True)]
    reduce_sum x19 -> x0, other arithmetic: 68.5 us -> none  [the longest x8 59.3 us: attend_inner(): running_sum = running_sum * fading + jnp.sum(probability, axis=-1)]
    dynamic_slice x32 -> x5, local copies, waits for them, and re-layouts: 32.1 us -> 3.86 us  [share(): return lax.dynamic_slice_in_dim(a, group * width, width, a.ndim - 1)]
    unnamed x122 -> x69, local copies, waits for them, and re-layouts: 38.1 us -> 12.8 us
  transfers between devices with their start and end apart: 15 -> 15, of which waited for: 12 -> 12; matrix products, arithmetic and copies ran while one was open for 17% -> 4% of each run, Pallas kernels for 0% -> 11%
where the time goes in v1:
time: 1190 us
  waiting for transfers between devices  811 us (68%)
  Pallas kernels  173 us (15%)
  blocking collectives  134 us (11%)
  local copies, waits for them, and re-layouts  34.5 us (3%)
  other arithmetic  20.3 us (2%)
  between operations  14.5 us (1%)
    reduce_scatter x6, waiting for transfers between devices, scatter(): lax.psum_scatter(a, both, scatter_dimension=0, tiled=True)  450 us
    all_gather x6, waiting for transfers between devices, gather(): return lax.all_gather(a.astype(bf16), both, axis=0, tiled=True)  226 us
    pallas_call x1, Pallas kernels, retreat(): pl.pallas_call(partial(retreat_kernel, heads, chunks, 'ctx', repeat), out...  86.3 us
    unnamed x2, blocking collectives  84.3 us
    reduce_scatter x1, waiting for transfers between devices, on_device(): dx = lax.psum_scatter(dx, 'ctx', scatter_dimension=0, tiled=True)[0]  69.5 us
    all_gather x1, waiting for transfers between devices, on_device(): x_all = lax.all_gather(x, 'ctx', axis=0, tiled=True)  62.6 us
    pallas_call x1, Pallas kernels, attend(): pl.pallas_call(partial(attend_kernel, heads, chunks, 'ctx', repeat), out_...  50.1 us
    pallas_call x1, Pallas kernels, middle(): pl.pallas_call(middle_kernel, out_shape=(shape((rows, model), f32), shape...  37 us
  transfers between devices with their start and end apart: 15, of which 12 were waited for; matrix products, arithmetic and copies ran while one was open for 4% of the time, Pallas kernels for 11%

profile of v1, /device:TPU:0, one launch (start us, length us, event | category | flops | bytes accessed | tf_op | source)
XLA Modules:
  0.0 1191.3 jit_solution(1314059106079963032)
XLA Ops:
  7.4 1.6 convert_element_type.86
  9.1 1.5 convert_element_type.85
  10.6 1.5 convert_element_type.87
  12.2 0.5 all-gather.23.cloned.1.call-update
  12.8 1.5 convert_element_type.91
  14.4 0.7 convert_element_type.92
  15.2 0.7 convert_element_type.93
  18.0 42.4 %all-reduce.19 = (bf16[768]{0:T(1024)(128)(2,1)S(1)}, bf16[768]{0:T(1024)(128)(2,1)S(1)}, bf16[768]{0:T(1024)(128)(2,1)S(1)}, bf16[768]{0:T(1024)(128)(2,1)S(1)}...) all-reduce(bf16[768]{0:T(1024)(128)(2,1)S(1)} %dynamic-update-slice, ...), channel_id=1, replica_groups=mesh['seq'=4,'ctx'=8] {'seq','ctx'}, use_global_device_ids=true, to_apply=%add.1 | all-reduce | flops 9216 | bytes 36864
  60.5 12.7 %all-gather.2 = s32[8,1,512]{2,1,0:T(1,128)S(1)} all-gather(s32[1,1,512]{2,1,0:T(1,128)S(1)} %bitcast.31), channel_id=1, replica_groups=mesh['seq'=4,'ctx'=8] {'ctx'}, dimensions={0}, use_global_device_ids=true | all-gather | bytes 18432 | tf_op jit(solution)/shard_map/all_gather | solution.py:615
  73.2 0.6 copy.40
  73.8 12.7 %all-gather.1 = s32[8,1,512]{2,1,0:T(1,128)S(1)} all-gather(s32[1,1,512]{2,1,0:T(1,128)S(1)} %bitcast.32), channel_id=1, replica_groups=mesh['seq'=4,'ctx'=8] {'ctx'}, dimensions={0}, use_global_device_ids=true | all-gather | bytes 18432 | tf_op jit(solution)/shard_map/all_gather | solution.py:614
  86.5 0.6 copy.41
  87.3 1.2 constant_dynamic-slice_fusion.1
  88.5 37.1 %all-gather.11.cloned.1.call-done = bf16[768,768]{1,0:T(8,128)(2,1)} async-done(((bf16[24,768]{1,0:T(8,128)(2,1)}), bf16[768,768]{1,0:T(8,128)(2,1)}) %all-gather.11.cloned.1.call-update) | async-done | bytes 1179664 | tf_op jit(solution)/shard_map/all_gather | solution.py:596
  125.6 1.2 constant_dynamic-slice_fusion.2
  126.9 55.5 %all-gather.15.cloned.1.call-done = bf16[768,768]{1,0:T(8,128)(2,1)} async-done(((bf16[24,768]{1,0:T(8,128)(2,1)}), bf16[768,768]{1,0:T(8,128)(2,1)}) %all-gather.15.cloned.1.call-update) | async-done | bytes 1179664 | tf_op jit(solution)/shard_map/all_gather | solution.py:596
  182.4 1.2 constant_dynamic-slice_fusion
  183.6 1.3 maximum_maximum_fusion.w_ref
  185.0 62.6 %all-gather.23.cloned.1.call-done = bf16[1,4096,768]{2,1,0:T(8,128)(2,1)} async-done(((bf16[1,512,768]{2,1,0:T(8,128)(2,1)}), bf16[1,4096,768]{2,1,0:T(8,128)(2,1)}) %all-gather.23.cloned.1.call-update) | async-done | bytes 6291472 | tf_op jit(solution)/shard_map/all_gather | solution.py:613
  247.6 0.8 broadcast_in_dim.22.bias_ref
  248.4 50.1 %attend.1 = (bf16[3,4864,64]{2,1,0:T(8,128)(2,1)}, bf16[192,4096]{1,0:T(8,128)(2,1)}, bf16[192,2048]{1,0:T(8,128)(2,1)}, f32[192,2048]{1,0:T(8,128)}, bf16[4,192,512]{2,1,0:T(8,128)(2,1)}, /*index=5*/f32[8,2048]{1,0:T(8,128)}) custom-call(bf16[4096,768]{1,0:T(8,128)(2,1)} %bitcast.20, bf16[768,640]{1,0:T(8,128)(2,1)} %maximum_maximum_fusion.w_ref, ...), custom_call_target="tpu_custom_call" | custom-call | tf_op jit(solution)/shard_map/attend/pallas_call | solution.py:188
  298.5 3.5 all-to-all-start
  302.3 0.6 stack.55.small_ref
  302.9 1.0 all-gather.17.cloned.1.call-done.wo_ref
  303.9 67.2 %all-gather.19.cloned.1.call-done.w1_ref = bf16[768,3072]{1,0:T(8,128)(2,1)} async-done(((bf16[24,3072]{1,0:T(8,128)(2,1)}), bf16[768,3072]{1,0:T(8,128)(2,1)}) %all-gather.19.cloned.1.call-update) | async-done | bytes 4718608 | tf_op jit(solution)/shard_map/all_gather | solution.py:596
  371.1 65.5 %all-gather.21.cloned.1.call-done.w2_ref = bf16[3072,768]{1,0:T(8,128)(2,1)} async-done(((bf16[96,768]{1,0:T(8,128)(2,1)}), bf16[3072,768]{1,0:T(8,128)(2,1)}) %all-gather.21.cloned.1.call-update) | async-done | bytes 4718608 | tf_op jit(solution)/shard_map/all_gather | solution.py:596
  436.7 0.7 broadcast_in_dim.23.b1_ref
  437.6 37.0 %middle.1 = (f32[512,768]{1,0:T(8,128)}, f32[512,768]{1,0:T(8,128)}, bf16[4,192,512]{2,1,0:T(8,128)(2,1)}, bf16[768,768]{1,0:T(8,128)(2,1)}, bf16[768,3072]{1,0:...) custom-call(bf16[4,192,512]{2,1,0:T(8,128)(2,1)} %copy-done.3, ...), custom_call_target="tpu_custom_call" | custom-call | tf_op jit(solution)/shard_map/middle/pallas_call | solution.py:551
  474.7 1.1 copy-done.5
  475.7 23.9 %all_to_all.10.do_ref = bf16[4,192,512]{2,1,0:T(8,128)(2,1)} all-to-all(bf16[4,192,512]{2,1,0:T(8,128)(2,1)S(1)} %copy-done.5), channel_id=1, replica_groups={{0,2,4,6},{1,3,5,7},{8,10,12,14},{9,11,13,15},{16,18,20,22},{17,19,21,2..., dimensions={0} | all-to-all | bytes 1572864 | tf_op jit(solution)/shard_map/all_to_all | solution.py:620
  499.7 86.3 %retreat.1 = (bf16[8,512,768]{2,1,0:T(8,128)(2,1)}, bf16[768,640]{1,0:T(8,128)(2,1)}, f32[8,384]{1,0:T(8,128)}) custom-call(bf16[4096,768]{1,0:T(8,128)(2,1)} %bitcast.21, bf16[768,640]{1,0:T(8,128)(2,1)} %maximum_maximum_fusion.w_ref, bf16[3,4864,64]{2,1,0:T(8,128)(2,1)} %get-tuple-element.37.k_ref, bf16[192,4096]{1,0:T(8,128)(2,1)} %get-tuple-element.38.v_ref, ...), custom_call_target="tpu_custom_call" | custom-call | tf_op jit(solution)/shard_map/retreat/pallas_call | solution.py:413
  586.0 1.5 fusion.1
  587.5 3.9 dynamic_update_slice.15
  591.5 1.0 copy-done.1
  592.6 3.9 dynamic_update_slice.17
  596.6 1.0 copy-done.2
  598.0 3.9 dynamic_update_slice.18
  601.9 1.0 copy-done
  603.6 0.7 reduce-scatter.20.cloned.1.call-update
  604.9 0.9 slice.44
  605.9 0.8 fusion.2
  607.1 41.9 %all-reduce.18 = (f32[768]{0:T(1024)S(1)}, f32[768]{0:T(1024)S(1)}, f32[768]{0:T(1024)S(1)}, f32[768]{0:T(1024)S(1)}, f32[768]{0:T(1024)S(1)}, /*index=5*/f32[30...) all-reduce(f32[768]{0:T(1024)S(1)} %dynamic_update_slice.16, ...), channel_id=5, replica_groups=mesh['seq'=4,'ctx'=8] {'seq','ctx'}, use_global_device_ids=true, to_apply=%region_2.3.clone | all-reduce | flops 9216 | bytes 73728
  649.0 0.6 dynamic-slice
  649.6 0.6 dynamic-slice.1
  650.2 0.6 dynamic-slice.2
  650.8 0.6 dynamic-slice.3
  651.4 0.6 dynamic-slice.4
  652.0 0.6 dynamic-slice.6
  652.5 0.6 dynamic-slice.7
  653.1 0.6 dynamic-slice.8
  653.7 0.6 dynamic-slice.5
  654.3 1.4 convert_element_type.107
  655.7 31.1 %reduce-scatter.10.cloned.1.call-done = bf16[24,768]{1,0:T(8,128)(2,1)} async-done(((bf16[768,768]{1,0:T(8,128)(2,1)}), bf16[24,768]{1,0:T(8,128)(2,1)}) %reduce-scatter.10.cloned.1.call-update) | async-done | bytes 36880 | tf_op jit(solution)/shard_map/reduce_scatter | solution.py:634
  686.8 1.4 convert_element_type.104
  688.2 98.8 %reduce-scatter.12.cloned.1.call-done = bf16[24,768]{1,0:T(8,128)(2,1)} async-done(((bf16[768,768]{1,0:T(8,128)(2,1)}), bf16[24,768]{1,0:T(8,128)(2,1)}) %reduce-scatter.12.cloned.1.call-update) | async-done | bytes 36880 | tf_op jit(solution)/shard_map/reduce_scatter | solution.py:634
  787.0 1.4 convert_element_type.105
  788.4 98.9 %reduce-scatter.14.cloned.1.call-done = bf16[24,768]{1,0:T(8,128)(2,1)} async-done(((bf16[768,768]{1,0:T(8,128)(2,1)}), bf16[24,768]{1,0:T(8,128)(2,1)}) %reduce-scatter.14.cloned.1.call-update) | async-done | bytes 36880 | tf_op jit(solution)/shard_map/reduce_scatter | solution.py:634
  887.3 1.4 convert_element_type.106
  888.7 110.1 %reduce-scatter.18.cloned.1.call-done = bf16[24,3072]{1,0:T(8,128)(2,1)} async-done(((bf16[768,3072]{1,0:T(8,128)(2,1)}), bf16[24,3072]{1,0:T(8,128)(2,1)}) %reduce-scatter.18.cloned.1.call-update) | async-done | bytes 147472 | tf_op jit(solution)/shard_map/reduce_scatter | solution.py:634
  998.8 1.6 convert_element_type.108
  1000.4 110.8 %reduce-scatter.20.cloned.1.call-done = bf16[96,768]{1,0:T(8,128)(2,1)} async-done(((bf16[3072,768]{1,0:T(8,128)(2,1)}), bf16[96,768]{1,0:T(8,128)(2,1)}) %reduce-scatter.20.cloned.1.call-update) | async-done | bytes 147472 | tf_op jit(solution)/shard_map/reduce_scatter | solution.py:634
  1111.3 1.6 convert_element_type.109
  1112.9 69.5 %reduce-scatter.8.cloned.1.call-done = bf16[1,512,768]{2,1,0:T(8,128)(2,1)} async-done(((bf16[8,512,768]{2,1,0:T(8,128)(2,1)}), bf16[1,512,768]{2,1,0:T(8,128)(2,1)}) %reduce-scatter.8.cloned.1.call-update) | async-done | bytes 786448 | tf_op jit(solution)/shard_map/reduce_scatter | solution.py:626
  1182.4 2.4 fusion
  (112 shorter events, 5.5 us)
Async XLA Ops:
  7.2 7.2 copy-start.6
  7.2 7.9 copy-start.7
  7.2 8.7 copy-start.11
  7.2 8.7 copy-start.12
  7.2 8.7 copy-start.13
  7.2 8.7 copy-start.14
  7.3 8.7 copy-start.15
  7.3 8.7 copy-start.16
  7.3 8.7 copy-start.17
  7.3 8.7 copy-start.18
  7.3 8.8 copy-start.19
  7.3 53.2 %copy-start.9 = (s32[1,512]{1,0:T(1,128)S(1)}, s32[1,512]{1,0:T(1,128)}, u32[]{:S(2)}) copy-start(s32[1,512]{1,0:T(1,128)} %param.21) | copy-start | bytes 6148
  7.3 66.5 %copy-start.10 = (s32[1,512]{1,0:T(1,128)S(1)}, s32[1,512]{1,0:T(1,128)}, u32[]{:S(2)}) copy-start(s32[1,512]{1,0:T(1,128)} %param.20) | copy-start | bytes 6148
  7.3 79.9 %all-gather.13.cloned.1.call-start = ((), (), s32[]{:S(2)}) async-start(), calls=%async_computation.10 | async-start | bytes 1216512 | tf_op jit(solution)/shard_map/all_gather | solution.py:596
  9.0 116.6 %all-gather.11.cloned.1.call-start = ((), (), s32[]{:S(2)}) async-start(), calls=%async_computation.9 | async-start | bytes 1216512 | tf_op jit(solution)/shard_map/all_gather | solution.py:596
  10.6 171.8 %all-gather.15.cloned.1.call-start = ((), (), s32[]{:S(2)}) async-start(), calls=%async_computation.11 | async-start | bytes 1216512 | tf_op jit(solution)/shard_map/all_gather | solution.py:596
  12.2 235.4 %all-gather.23.cloned.1.call-start = ((), (), s32[]{:S(2)}) async-start(), calls=%async_computation.22 | async-start | bytes 7077888 | tf_op jit(solution)/shard_map/all_gather | solution.py:613
  12.8 291.1 %all-gather.17.cloned.1.call-start = ((), (), s32[]{:S(2)}) async-start(), calls=%async_computation.12 | async-start | bytes 1216512 | tf_op jit(solution)/shard_map/all_gather | solution.py:596
  14.3 356.8 %all-gather.19.cloned.1.call-start = ((), (), s32[]{:S(2)}) async-start(), calls=%async_computation.13 | async-start | bytes 4866048 | tf_op jit(solution)/shard_map/all_gather | solution.py:596
  15.1 421.6 %all-gather.21.cloned.1.call-start = ((), (), s32[]{:S(2)}) async-start(), calls=%async_computation.14 | async-start | bytes 4866048 | tf_op jit(solution)/shard_map/all_gather | solution.py:596
  298.5 138.2 %all-to-all-start = ((bf16[4,192,512]{2,1,0:T(8,128)(2,1)}), bf16[4,192,512]{2,1,0:T(8,128)(2,1)S(1)}, u32[]{:S(2)}, u32[]{:S(2)}) async-start(bf16[4,192,512]{2,1,0:T(8,128)(2,1)} %get-tuple-element.34), calls=%async_computation | async-start | bytes 1572864 | tf_op jit(solution)/shard_map/all_to_all | solution.py:620
  302.0 352.3 %reduce-scatter.16.cloned.1.call-start = ((), (), s32[]{:S(2)}) async-start(), calls=%async_computation.19 | async-start | bytes 1216512 | tf_op jit(solution)/shard_map/reduce_scatter | solution.py:634
  436.7 0.9 copy-start.3
  474.6 1.1 copy-start.5
  474.6 212.2 %reduce-scatter.10.cloned.1.call-start = ((), (), s32[]{:S(2)}) async-start(), calls=%async_computation.16 | async-start | bytes 1216512 | tf_op jit(solution)/shard_map/reduce_scatter | solution.py:634
  591.5 1.0 copy-start.1
  592.5 194.5 %reduce-scatter.12.cloned.1.call-start = ((), (), s32[]{:S(2)}) async-start(), calls=%async_computation.17 | async-start | bytes 1216512 | tf_op jit(solution)/shard_map/reduce_scatter | solution.py:634
  596.5 1.0 copy-start.2
  597.6 289.7 %reduce-scatter.14.cloned.1.call-start = ((), (), s32[]{:S(2)}) async-start(), calls=%async_computation.18 | async-start | bytes 1216512 | tf_op jit(solution)/shard_map/reduce_scatter | solution.py:634
  601.9 1.0 copy-start
  603.0 395.8 %reduce-scatter.18.cloned.1.call-start = ((), (), s32[]{:S(2)}) async-start(), calls=%async_computation.20 | async-start | bytes 4866048 | tf_op jit(solution)/shard_map/reduce_scatter | solution.py:634
  603.6 507.7 %reduce-scatter.20.cloned.1.call-start = ((), (), s32[]{:S(2)}) async-start(), calls=%async_computation.21 | async-start | bytes 4866048 | tf_op jit(solution)/shard_map/reduce_scatter | solution.py:634
  604.3 578.1 %reduce-scatter.8.cloned.1.call-start = ((), (), s32[]{:S(2)}) async-start(), calls=%async_computation.15 | async-start | bytes 7077888 | tf_op jit(solution)/shard_map/reduce_scatter | solution.py:626
  604.3 1.4 copy-start.8
  604.4 578.0 %copy-start.4 = (f32[512,768]{1,0:T(8,128)S(1)}, f32[512,768]{1,0:T(8,128)}, u32[]{:S(2)}) copy-start(f32[512,768]{1,0:T(8,128)} %get-tuple-element.36) | copy-start | bytes 4718596
Sparse Core Ops, SparseCore 0:
  11.8 57.2 all-gather.12
  72.6 52.9 all-gather.10
  129.2 53.1 all-gather.14
  183.9 63.6 all-gather.22
  251.0 52.8 all-gather.16
  307.3 63.7 all-gather.18
  374.2 62.4 all-gather.20
  474.8 95.0 reduce-scatter.15
  592.6 94.1 reduce-scatter.9
  691.8 95.1 reduce-scatter.11
  792.1 95.2 reduce-scatter.13
  892.7 106.0 reduce-scatter.17
  1005.2 106.0 reduce-scatter.19
  1113.4 68.8 reduce-scatter.7

commit v2 on v1

--- a/solution.py
+++ b/solution.py
@@ -28,10 +28,10 @@
     return lax.dot_general(a, b, (((1,), (0,)), ((), ())), preferred_element_type=jnp.float32)
 
 
-def code_columns(seg_ref, val_ref, kcode, pad):
-    count, width = seg_ref.shape
+def code_columns(code_ref, kcode, pad):
+    count, width = code_ref.shape
     for i in range(count):
-        code = (seg_ref[i : i + 1, :] * 2 + val_ref[i : i + 1, :]).astype(jnp.float32)
+        code = code_ref[i : i + 1, :].astype(jnp.float32)
         for j in range(width // LANES):
             piece = code[:, j * LANES : (j + 1) * LANES]
             at = i * width + j * LANES
@@ -39,13 +39,29 @@
     kcode[count * width :, :] = jnp.full((pad, LANES), -1.0, jnp.float32)
 
 
+def unshard(vec, at, each):
+    devices = vec.shape[0]
+    shard = vec[:, at : at + each].astype(jnp.bfloat16)
+    size = devices * each
+    owner = lambda shape, axis: jnp.floor(
+        (lax.broadcasted_iota(jnp.int32, shape, axis).astype(jnp.float32) + 0.5) / each
+    )
+    column = lax.broadcasted_iota(jnp.int32, (each, size), 1).astype(jnp.float32)
+    inner = column - owner((each, size), 1) * each
+    place = lax.broadcasted_iota(jnp.int32, (each, size), 0).astype(jnp.float32)
+    repeated = nn(shard, (inner == place).astype(jnp.bfloat16))
+    device = lax.broadcasted_iota(jnp.int32, (devices, size), 0).astype(jnp.float32)
+    return jnp.sum(jnp.where(owner((devices, size), 1) == device, repeated, 0.0), axis=0, keepdims=True)
+
+
 def total(values):
     return jnp.sum(values.astype(jnp.float32)).astype(jnp.int32)
 
 
-def key_range(seg_ref, val_ref, block, start):
-    seg = seg_ref[...]
-    val = val_ref[...]
+def key_range(code_ref, block, start):
+    code = code_ref[...]
+    seg = lax.shift_right_logical(code, 1)
+    val = code & 1
     count, width = seg.shape
     position = lax.broadcasted_iota(jnp.int32, (count, width), 0) * width + lax.broadcasted_iota(
         jnp.int32, (count, width), 1
@@ -72,19 +88,32 @@
 
 def attend_kernel(
     heads, chunks, ctx_axis, repeat,
-    x_ref, w_ref, bias_ref, seg_ref, val_ref,
-    k_out, v_out, q_out, of_out, ob_out, lse_out,
+    x_ref, w_ref, vec_ref, codes_ref,
+    k_out, v_out, q_out, of_out, ob_out, lse_out, code_ref,
     kcode, q_ext, k_ext, v_ext, s_even, s_odd,
 ):
     width = heads * DH
     length = x_ref.shape[0]
     rows = length // (chunks * repeat)
     place = lax.rem(lax.axis_index(ctx_axis), repeat)
-    code_columns(seg_ref, val_ref, kcode, PAD)
+    code_ref[...] = codes_ref[:, 0, :]
+    code_columns(code_ref, kcode, PAD)
     wt = w_ref[...].astype(jnp.float32).T.astype(jnp.bfloat16)
     wq, wv = wt[:width], wt[2 * width : 3 * width]
-    bias_q = bias_ref[0:width, 0:1]
-    bias_v = bias_ref[width : 2 * width, 0:1]
+    vec = vec_ref[:, 0, :]
+    each = x_ref.shape[1] // vec.shape[0]
+    group = lax.axis_index(ctx_axis) // repeat
+
+    def bias_column(which):
+        whole = unshard(vec, which * each, each)
+        row = jnp.zeros((1, width), jnp.float32)
+        for k in range(chunks):
+            row = row + jnp.where(group == k, whole[:, k * width : (k + 1) * width], 0.0)
+        extra = -width % LANES
+        row = jnp.concatenate([row, jnp.zeros((1, extra), jnp.float32)], axis=1)
+        return jnp.broadcast_to(row, (LANES, width + extra)).T[0:width, 0:1]
+
+    bias_q, bias_v = bias_column(6), bias_column(7)
 
     def keys(i, carry):
         at = pl.multiple_of(i * rows, LANES)
@@ -125,10 +154,10 @@
         chunk = i // per_chunk
         inner = pl.multiple_of((i - chunk * per_chunk) * BQ, LANES)
         start = (chunk * repeat + place) * rows + inner
-        origin, blocks, clear_from, clear_to = key_range(seg_ref, val_ref, BQ, start)
+        origin, blocks, clear_from, clear_to = key_range(code_ref, BQ, start)
         at = pl.multiple_of(i * BQ, LANES)
         which = chunk * repeat + place
-        target = (seg_ref[pl.ds(which, 1), pl.ds(inner, BQ)] * 2 + 1).astype(jnp.float32)
+        target = (code_ref[pl.ds(which, 1), pl.ds(inner, BQ)] | 1).astype(jnp.float32)
 
         def scores(slot, key_at):
             for h in range(heads):
@@ -177,10 +206,10 @@
     lax.fori_loop(0, chunks * per_chunk, block, 0)
 
 
-def attend(x, w, bias, seg, val, heads, chunks):
+def attend(x, w, vec, codes, heads, chunks):
     length = x.shape[0]
     width = heads * DH
-    count, rows = seg.shape
+    count, _, rows = codes.shape
     repeat = count // chunks
     mine = chunks * rows
     shape = jax.ShapeDtypeStruct
@@ -194,9 +223,10 @@
             shape((width, mine), jnp.float32),
             shape((chunks, width, rows), jnp.bfloat16),
             shape((8, mine), jnp.float32),
+            shape((count, rows), jnp.int32),
         ),
-        in_specs=[whole] * 5,
-        out_specs=(whole,) * 6,
+        in_specs=[whole] * 4,
+        out_specs=(whole,) * 7,
         scratch_shapes=[
             pltpu.VMEM((length + PAD, LANES), jnp.float32),
             pltpu.VMEM((heads, 2 * DH, mine), jnp.bfloat16),
@@ -207,7 +237,7 @@
         ],
         compiler_params=pltpu.CompilerParams(vmem_limit_bytes=VMEM_LIMIT),
         name="attend",
-    )(x, w, bias, seg, val)
+    )(x, w, vec, codes)
 
 
 def tn(a, b):
@@ -231,7 +261,7 @@
 
 def retreat_kernel(
     heads, chunks, ctx_axis, repeat,
-    x_ref, w_ref, k_ref, v_ref, q_ref, o_ref, lse_ref, do_ref, seg_ref, val_ref,
+    x_ref, w_ref, k_ref, v_ref, q_ref, o_ref, lse_ref, do_ref, code_ref,
     dx_out, dw_out, db_out,
     krow, target, q_ext, kt_ext, v_ext, do_ext, do_rows, dq, dkv,
     s_even, s_odd, g_even, g_odd, dw, x_slot, dx_slot, in_sem, out_sem, v_sem,
@@ -263,7 +293,7 @@
     for copy in values:
         copy.start()
     for i in range(chunks * repeat):
-        code = (seg_ref[i : i + 1, :] * 2 + val_ref[i : i + 1, :]).astype(jnp.float32)
+        code = code_ref[i : i + 1, :].astype(jnp.float32)
         krow[:, i * rows : (i + 1) * rows] = jnp.broadcast_to(code, (8, rows))
     krow[:, length:] = jnp.full((8, PAD), -1.0, jnp.float32)
 
@@ -286,7 +316,7 @@
     def queries(i, carry):
         at = pl.ds(pl.multiple_of(i * rows, LANES), rows)
         which = i * repeat + place
-        code = (seg_ref[pl.ds(which, 1), :] * 2 + 1).astype(jnp.float32)
+        code = (code_ref[pl.ds(which, 1), :] | 1).astype(jnp.float32)
         for j in range(rows // LANES):
             piece = code[:, j * LANES : (j + 1) * LANES]
             target[pl.ds(pl.multiple_of(i * rows + j * LANES, LANES), LANES), :] = jnp.broadcast_to(
@@ -312,7 +342,7 @@
         chunk = i // per_chunk
         inner = (i - chunk * per_chunk) * BQ
         start = (chunk * repeat + place) * rows + inner
-        origin, blocks, clear_from, clear_to = key_range(seg_ref, val_ref, BQ, start)
+        origin, blocks, clear_from, clear_to = key_range(code_ref, BQ, start)
         at = pl.ds(pl.multiple_of(i * BQ, LANES), BQ)
 
         def scores(s_slot, g_slot, key_at):
@@ -401,10 +431,10 @@
     dw_out[...] = dw[...].T.astype(bf16)
 
 
-def retreat(x, w, k, v, q, o, lse, do, seg, val, heads, chunks):
+def retreat(x, w, k, v, q, o, lse, do, codes, heads, chunks):
     length, model = x.shape
     width = heads * DH
-    count, rows = seg.shape
+    count, rows = codes.shape
     repeat = count // chunks
     mine = chunks * rows
     shape = jax.ShapeDtypeStruct
@@ -417,7 +447,7 @@
             shape((model, w.shape[1]), bf16),
             shape((8, 2 * width), f32),
         ),
-        in_specs=[whole if i not in (0, 3) else pl.BlockSpec(memory_space=pl.ANY) for i in range(10)],
+        in_specs=[whole if i not in (0, 3) else pl.BlockSpec(memory_space=pl.ANY) for i in range(9)],
         out_specs=(pl.BlockSpec(memory_space=pl.ANY), whole, whole),
         scratch_shapes=[
             pltpu.VMEM((8, length + PAD), f32),
@@ -441,7 +471,7 @@
         ],
         compiler_params=pltpu.CompilerParams(vmem_limit_bytes=VMEM_LIMIT),
         name="retreat",
-    )(x, w, k, v, q, o, lse, do, seg, val)
+    )(x, w, k, v, q, o, lse, do, codes)
 
 
 EPSILON = 1e-12
@@ -476,14 +506,19 @@
 
 
 def middle_kernel(
-    o_ref, x_ref, cot_ref, wo_ref, w1_ref, w2_ref, small_ref, b1_ref,
+    o_ref, x_ref, cot_ref, wo_ref, w1_ref, w2_ref, vec_ref,
     out_ref, e1_ref, do_ref, dwo_ref, dw1_ref, dw2_ref, dsmall_ref, db1_ref,
-    act, slope, y1_ref, normal_ref, r2_ref, y1t_ref, grad_ref,
+    act, slope, y1_ref, normal_ref, r2_ref, y1t_ref, grad_ref, small_ref, b1_ref,
 ):
     bf16 = jnp.bfloat16
     groups, width, rows = o_ref.shape
     hidden_width = w1_ref.shape[1]
     steps = hidden_width // FF_BLOCK
+    vec = vec_ref[:, 0, :]
+    each = x_ref.shape[1] // vec.shape[0]
+    for i in range(6):
+        small_ref[i : i + 1, :] = unshard(vec, i * each, each)
+    b1_ref[0:1, :] = unshard(vec, 8 * each, hidden_width // vec.shape[0])
     row = lambda i: small_ref[i : i + 1, :]
     ones = jnp.ones((8, rows), bf16)
     o = o_ref[...].reshape(groups * width, rows)
@@ -541,7 +576,7 @@
     do_ref[...] = nt(wo_ref[...], r1).astype(bf16).reshape(groups, width, rows)
 
 
-def middle(o, x, cot, wo, w1, w2, small, b1):
+def middle(o, x, cot, wo, w1, w2, vec):
     groups, width, rows = o.shape
     model = x.shape[1]
     hidden_width = w1.shape[1]
@@ -560,7 +595,7 @@
             shape((8, model), f32),
             shape((8, hidden_width), f32),
         ),
-        in_specs=[whole] * 8,
+        in_specs=[whole] * 7,
         out_specs=(whole,) * 8,
         scratch_shapes=[
             pltpu.VMEM((rows, hidden_width), bf16),
@@ -570,10 +605,807 @@
             pltpu.VMEM((rows, model), bf16),
             pltpu.VMEM((model, rows), bf16),
             pltpu.VMEM((rows, model), f32),
+            pltpu.VMEM((8, model), f32),
+            pltpu.VMEM((8, hidden_width), f32),
         ],
         compiler_params=pltpu.CompilerParams(vmem_limit_bytes=VMEM_LIMIT),
         name="middle",
-    )(o, x, cot, wo, w1, w2, small, b1)
+    )(o, x, cot, wo, w1, w2, vec)
+
+
+MESH = pl.DeviceIdType.MESH
+
+
+class Sender:
+    def __init__(self, send_sems, recv_sems):
+        self.send_sems, self.recv_sems, self.used, self.open = send_sems, recv_sems, 0, []
+
+    def copy(self, source, target, device, when=None, until=None):
+        index = self.used
+        self.used += 1
+        one = pltpu.make_async_remote_copy(
+            src_ref=source,
+            dst_ref=target,
+            send_sem=self.send_sems.at[index],
+            recv_sem=self.recv_sems.at[index],
+            device_id=device,
+            device_id_type=MESH,
+        )
+        if when is None:
+            one.start()
+        else:
+            pl.when(when)(one.start)
+        self.open.append((one, when))
+
+        def arrive():
+            if until is None:
+                one.wait_recv()
+            else:
+                pl.when(until)(one.wait_recv)
+
+        return arrive
+
+    def finish(self):
+        for one, when in self.open:
+            if when is None:
+                one.wait_send()
+            else:
+                pl.when(when)(one.wait_send)
+
+
+def greet(seqs, count):
+    s, c = lax.axis_index("seq"), lax.axis_index("ctx")
+    barrier = pltpu.get_barrier_semaphore()
+    for d in range(1, count):
+        pl.semaphore_signal(barrier, inc=1, device_id=(s, lax.rem(c + d, count)), device_id_type=MESH)
+    for d in range(1, seqs):
+        pl.semaphore_signal(barrier, inc=1, device_id=(lax.rem(s + d, seqs), c), device_id_type=MESH)
+    pl.semaphore_wait(barrier, count - 1 + seqs - 1)
+
+
+def cube_steps(seqs, turn):
+    bits = seqs.bit_length() - 1
+    masks = []
+    for j in range(bits):
+        bit = lax.rem(j + turn, bits)
+        mask = 0
+        for k in range(bits):
+            mask = mask + jnp.where(bit == k, 1 << k, 0)
+        masks.append(mask)
+    return masks
+
+
+def across(s, mask):
+    return s + mask * (1 - 2 * lax.rem(s // mask, 2))
+
+
+def block_mates(rows):
+    mates = 1
+    while (mates * rows) % 16:
+        mates *= 2
+    return mates
+
+
+def collect_kernel(
+    seqs, count, chunks, semaphores,
+    wq_ref, wk_ref, wv_ref, wo_ref, w1_ref, w2_ref, x_ref, code_ref, vec_ref,
+    w_out, wo_out, w1_out, w2_out, x_out, code_out, vec_out,
+    stage4, stage1, stage2, flat4, flat1, flat2, low4, low1, low2, share4,
+    send_sems, recv_sems, here_sems,
+):
+    s, c = lax.axis_index("seq"), lax.axis_index("ctx")
+    bf16 = jnp.bfloat16
+    small_rows, model = wq_ref.shape
+    tall_rows = w2_ref.shape[0]
+    wide = w1_ref.shape[1]
+    mates = block_mates(small_rows)
+    blocks = count // mates
+    b, i = c // mates, lax.rem(c, mates)
+    turn = lax.rem(c, 2)
+    repeat = count // chunks
+    g, r = c // repeat, lax.rem(c, repeat)
+    group_width = model // chunks
+    rows = x_ref.shape[0]
+    block_rows, block_tall = mates * small_rows, mates * tall_rows
+    sender = Sender(send_sems, recv_sems)
+    here = []
+
+    def move(source, target):
+        one = pltpu.make_async_copy(source, target, here_sems.at[len(here)])
+        one.start()
+        here.append(one)
+
+    greet(seqs, count)
+
+    shards = []
+    matrices = (wq_ref, wk_ref, wv_ref, wo_ref)
+    for d in range(1, mates):
+        other = (s, b * mates + lax.rem(i + d, mates))
+        for m in range(4):
+            shards.append(sender.copy(matrices[m], stage4.at[i, m], other))
+        shards.append(sender.copy(w1_ref, stage1.at[i], other))
+        shards.append(sender.copy(w2_ref, stage2.at[i], other))
+    for m in range(4):
+        stage4[i, m] = matrices[m][...]
+    stage1[i] = w1_ref[...]
+    stage2[i] = w2_ref[...]
+
+    codes, vecs = [], []
+    for d in range(1, count):
+        other = (s, lax.rem(c + d, count))
+        codes.append(sender.copy(code_ref, code_out.at[c], other))
+        vecs.append(sender.copy(vec_ref, vec_out.at[s * count + c], other))
+    move(code_ref, code_out.at[c])
+    move(vec_ref, vec_out.at[s * count + c])
+
+    def tokens_at(group, half):
+        start = (group * repeat + r) * rows + half * (rows // 2)
+        return pl.ds(pl.multiple_of(start, rows // 2), rows // 2)
+
+    mate_waits = []
+
+    def to_mates(source, group, half, when=None, until_group=None):
+        for d in range(1, repeat):
+            other = (s, g * repeat + lax.rem(r + d, repeat))
+            mate_waits.append(
+                sender.copy(source, x_out.at[tokens_at(group, half)], other, when, when)
+            )
+
+    half_rows = [pl.ds(h * (rows // 2), rows // 2) for h in range(2)]
+    for h in range(2):
+        to_mates(x_ref.at[half_rows[h]], g, h)
+        move(x_ref.at[half_rows[h]], x_out.at[tokens_at(g, h)])
+
+    for wait in shards:
+        wait()
+    for p in range(mates):
+        for m in range(4):
+            flat4[m, p * small_rows : (p + 1) * small_rows, :] = stage4[p, m]
+        flat1[p * small_rows : (p + 1) * small_rows, :] = stage1[p]
+        flat2[p * tall_rows : (p + 1) * tall_rows, :] = stage2[p]
+    for k in range(chunks):
+        part = slice(k * group_width, (k + 1) * group_width)
+        pieces = [flat4[m, :, part] for m in range(3)]
+        pieces.append(jnp.zeros((block_rows, w_out.shape[1] - 3 * group_width), jnp.float32))
+        share4[k] = jnp.concatenate(pieces, axis=1).astype(bf16)
+    low4[...] = flat4[3].astype(bf16)
+    low1[...] = flat1[...].astype(bf16)
+    low2[...] = flat2[...].astype(bf16)
+
+    def w_rows(seq, block, size):
+        start = (seq * blocks + block) * block_rows
+        return pl.ds(pl.multiple_of(start, block_rows), size * block_rows)
+
+    columns = []
+    for d in range(1, blocks):
+        to = lax.rem(b + d, blocks) * mates + i
+        columns.append(
+            sender.copy(share4.at[to // repeat], w_out.at[w_rows(s, b, 1)], (s, to))
+        )
+    move(share4.at[g], w_out.at[w_rows(s, b, 1)])
+
+    half_wide, half_model = wide // 2, model // 2
+    wide_at = pl.ds(pl.multiple_of(turn * half_wide, half_wide), half_wide)
+    model_at = pl.ds(pl.multiple_of(turn * half_model, half_model), half_model)
+
+    def tall_rows_at(seq, block, size):
+        start = (seq * blocks + block) * block_tall
+        return pl.ds(pl.multiple_of(start, block_tall), size * block_tall)
+
+    def big(seq, block, size):
+        return (
+            w1_out.at[w_rows(seq, block, size), wide_at],
+            w2_out.at[tall_rows_at(seq, block, size), model_at],
+            wo_out.at[w_rows(seq, block, size), model_at],
+        )
+
+    own = (low1.at[:, wide_at], low2.at[:, model_at], low4.at[:, model_at])
+    for source, target in zip(own, big(s, b, 1)):
+        move(source, target)
+    up, down = b * mates + mates + i, b * mates - mates + i
+    line = []
+    for t in range(blocks - 1):
+        for wait in line:
+            wait()
+        line = []
+        low_block, high_block = jnp.maximum(b - t, 0), jnp.minimum(b + t, blocks - 1)
+        sources = (own, own) if t == 0 else (big(s, low_block, 1), big(s, high_block, 1))
+        rising = (b - t >= 0) & (b + 1 < blocks)
+        falling = (b + t < blocks) & (b >= 1)
+        for source, target in zip(sources[0], big(s, low_block, 1)):
+            line.append(
+                sender.copy(source, target, (s, jnp.minimum(up, count - 1)), rising, b - 1 - t >= 0)
+            )
+        for source, target in zip(sources[1], big(s, high_block, 1)):
+            line.append(
+                sender.copy(source, target, (s, jnp.maximum(down, 0)), falling, b + 1 + t < blocks)
+            )
+
+    above, below = jnp.minimum((g + 1) * repeat + r, count - 1), jnp.maximum((g - 1) * repeat + r, 0)
+
+    def pass_on(t):
+        waits = []
+        low_group, high_group = jnp.maximum(g - t, 0), jnp.minimum(g + t, chunks - 1)
+        for h in range(2):
+            rise = x_ref.at[half_rows[h]] if t == 0 else x_out.at[tokens_at(low_group, h)]
+            fall = x_ref.at[half_rows[h]] if t == 0 else x_out.at[tokens_at(high_group, h)]
+            rising = (g - t >= 0) & (g + 1 < chunks)
+            falling = (g + t < chunks) & (g >= 1)
+            waits.append((
+                sender.copy(rise, x_out.at[tokens_at(low_group, h)], (s, above), rising, g - 1 - t >= 0),
+                sender.copy(
+                    fall, x_out.at[tokens_at(high_group, h)], (s, below), falling, g + 1 + t < chunks
+                ),
+            ))
+        return waits
+
+    def received(t, waits):
+        low_group, high_group = jnp.maximum(g - 1 - t, 0), jnp.minimum(g + 1 + t, chunks - 1)
+        for h in range(2):
+            waits[h][0]()
+            to_mates(x_out.at[tokens_at(low_group, h)], low_group, h, g - 1 - t >= 0)
+            waits[h][1]()
+            to_mates(x_out.at[tokens_at(high_group, h)], high_group, h, g + 1 + t < chunks)
+
+    x_waits = pass_on(0)
+
+    for wait in columns:
+        wait()
+    for one in here:
+        one.wait()
+    columns = []
+    for d in range(1, seqs):
+        to = (lax.rem(s + d, seqs), c)
+        slab = w_out.at[w_rows(s, 0, blocks)]
+        columns.append(sender.copy(slab, slab, to))
+    for wait in vecs:
+        wait()
+    vecs = []
+    for d in range(1, seqs):
+        to = (lax.rem(s + d, seqs), c)
+        slab = vec_out.at[pl.ds(s * count, count)]
+        vecs.append(sender.copy(slab, slab, to))
+    for wait in line:
+        wait()
+
+    sibling = (s, c + 1 - 2 * turn)
+    sibling_waits = []
+
+    def to_sibling(seq):
+        for piece in big(seq, 0, blocks):
+            sibling_waits.append(sender.copy(piece, piece, sibling))
+
+    masks = cube_steps(seqs, turn)
+    held = [s]
+    step = 0
+    for t in range(max(chunks - 1, len(masks) + 1)):
+        if t <= len(masks):
+            if t > 0:
+                for wait in plane:
+                    wait()
+            fresh = held if t == 0 else held[len(held) // 2 :]
+            plane = []
+            if t < len(masks):
+                partner = (across(s, masks[t]), c)
+                for seq in held:
+                    for piece in big(seq, 0, blocks):
+                        plane.append(sender.copy(piece, piece, partner))
+                held = held + [across(seq, masks[t]) for seq in held]
+            for seq in fresh:
+                to_sibling(seq)
+        if t < chunks - 1:
+            following = None
+            if t + 1 < chunks - 1:
+                for h in range(2):
+                    pass
+            received(t, x_waits)
+            if t + 1 < chunks - 1:
+                x_waits = pass_on(t + 1)
+    for wait in codes + vecs + columns + sibling_waits + mate_waits:
+        wait()
+    sender.finish()
+
+
+def collect(wq, wk, wv, wo, w1, w2, x, code, vec, chunks):
+    seqs, count = lax.axis_size("seq"), lax.axis_size("ctx")
+    small_rows, model = wq.shape
+    tall_rows, wide = w2.shape[0], w1.shape[1]
+    rows = x.shape[0]
+    mates = block_mates(small_rows)
+    blocks, repeat = count // mates, count // chunks
+    semaphores = (
+        6 * (mates - 1) + 2 * (count - 1) + 2 * (seqs - 1) + 7 * (blocks - 1)
+        + 3 * (seqs - 1) + 3 * seqs + 4 * (chunks - 1) + 2 * (2 * chunks - 1) * (repeat - 1)
+    )
+    devices = seqs * count
+    padded = -(-3 * (model // chunks) // LANES) * LANES
+    shape = jax.ShapeDtypeStruct
+    f32, bf16 = jnp.float32, jnp.bfloat16
+    vmem, far = pl.BlockSpec(memory_space=pltpu.VMEM), pl.BlockSpec(memory_space=pl.ANY)
+    block_rows, block_tall = mates * small_rows, mates * tall_rows
+    return pl.pallas_call(
+        partial(collect_kernel, seqs, count, chunks, semaphores),
+        out_shape=(
+            shape((model, padded), bf16),
+            shape((model, model), bf16),
+            shape((model, wide), bf16),
+            shape((tall_rows * devices, model), bf16),
+            shape((count * rows, model), bf16),
+            shape((count, 1, rows), jnp.int32),
+            shape((devices, 1, vec.shape[1]), f32),
+        ),
+        in_specs=[vmem] * 6 + [far] * 3,
+        out_specs=(far,) * 7,
+        scratch_shapes=[
+            pltpu.VMEM((mates, 4, small_rows, model), f32),
+            pltpu.VMEM((mates, small_rows, wide), f32),
+            pltpu.VMEM((mates, tall_rows, model), f32),
+            pltpu.VMEM((4, block_rows, model), f32),
+            pltpu.VMEM((block_rows, wide), f32),
+            pltpu.VMEM((block_tall, model), f32),
+            pltpu.VMEM((block_rows, model), bf16),
+            pltpu.VMEM((block_rows, wide), bf16),
+            pltpu.VMEM((block_tall, model), bf16),
+            pltpu.VMEM((chunks, block_rows, padded), bf16),
+            pltpu.SemaphoreType.DMA((semaphores,)),
+            pltpu.SemaphoreType.DMA((semaphores,)),
+            pltpu.SemaphoreType.DMA((8,)),
+        ],
+        compiler_params=pltpu.CompilerParams(
+            vmem_limit_bytes=VMEM_LIMIT, collective_id=1, has_side_effects=True
+        ),
+        name="collect",
+    )(wq, wk, wv, wo, w1, w2, x, code, vec)
+
+
+def added(*parts):
+    sum_of = parts[0].astype(jnp.float32)
+    for part in parts[1:]:
+        sum_of = sum_of + part.astype(jnp.float32)
+    return sum_of
+
+
+class Line:
+    def __init__(self, sender, place, size, device, pieces, landing):
+        self.sender, self.place, self.size, self.device = sender, place, size, device
+        self.pieces, self.landing = pieces, landing
+        self.waits = None
+
+    def send(self, t):
+        self.waits = []
+        for way in range(2):
+            rank = self.place if way == 0 else self.size - 1 - self.place
+            mirror = (lambda d: d) if way == 0 else (lambda d: self.size - 1 - d)
+            goal = jnp.clip(mirror(self.size - 1 - t + rank), 0, self.size - 1)
+            sends = rank <= t
+            receives = (rank >= 1) & (rank - 1 <= t)
+            to = jnp.clip(self.place + (1 - 2 * way), 0, self.size - 1)
+            waits = []
+            for source, target in zip(self.pieces(goal), self.landing(way, t)):
+                waits.append(self.sender.copy(source, target, self.device(to), sends, receives))
+            self.waits.append((receives, mirror, rank, waits))
+
+    def receive(self, t):
+        for way, (receives, mirror, rank, waits) in enumerate(self.waits):
+            goal = jnp.clip(mirror(self.size - 2 - t + rank), 0, self.size - 1)
+            pieces, landing = self.pieces(goal), self.landing(way, t)
+            for wait, piece, arrived in zip(waits, pieces, landing):
+                wait()
+
+                @pl.when(receives)
+                def _():
+                    piece[...] = added(piece[...], arrived[...]).astype(piece.dtype)
+
+
+def settle_kernel(
+    seqs, count, chunks,
+    dx_ref, dw_ref, dwo_ref, dw1_ref, dw2_ref, dsmall_ref, db1_ref, db_ref,
+    dx_out, dw_out, dwo_out, dw1_out, dw2_out, dsmall_out, db1_out,
+    dx_sum, dx_in, dx_line, sum1, sum2, sum4, in1, in2, in4, cube1, cube2, cube4,
+    line1, line2, line4, last1, last2, last4, w_mine, w_seq, w_block, w_mates, w_tmp,
+    small_in, b1_in, b_in, vec_seq,
+    send_sems, recv_sems, here_sems,
+):
+    s, c = lax.axis_index("seq"), lax.axis_index("ctx")
+    bf16 = jnp.bfloat16
+    rows, model = dx_out.shape
+    wide = dw1_ref.shape[1]
+    repeat = count // chunks
+    mates = w_mates.shape[0]
+    blocks = count // mates
+    block_rows, block_tall = dwo_out.shape[0], dw2_out.shape[0]
+    width = model // chunks
+    b, i = c // mates, lax.rem(c, mates)
+    g, r = c // repeat, lax.rem(c, repeat)
+    turn = lax.rem(c, 2)
+    half_wide, half_model = wide // 2, model // 2
+    slab_rows, slab_tall = blocks * block_rows, blocks * block_tall
+    sender = Sender(send_sems, recv_sems)
+    here = []
+
+    def move(source, target):
+        one = pltpu.make_async_copy(source, target, here_sems.at[len(here)])
+        one.start()
+        here.append(one)
+
+    greet(seqs, count)
+
+    dx_waits = []
+    for d in range(1, repeat):
+        to = lax.rem(r + d, repeat)
+        for k in range(chunks):
+            dx_waits.append(
+                sender.copy(dx_ref.at[k * repeat + to], dx_in.at[d - 1, k], (s, g * repeat + to))
+            )
+    for k in range(chunks):
+        move(dx_ref.at[k * repeat + r], dx_sum.at[k])
+
+    sibling = (s, c + 1 - 2 * turn)
+
+    def column_half(which):
+        wide_at = pl.ds(pl.multiple_of(which * half_wide, half_wide), half_wide)
+        model_at = pl.ds(pl.multiple_of(which * half_model, half_model), half_model)
+        return dw1_ref.at[:, wide_at], dw2_ref.at[:, model_at], dwo_ref.at[:, model_at]
+
+    half_waits = [
+        sender.copy(source, target, sibling)
+        for source, target in zip(column_half(1 - turn), (in1, in2, in4))
+    ]
+    for source, target in zip(column_half(turn), (sum1, sum2, sum4)):
+        move(source, target)
+
+    w_waits = []
+    for d in range(1, seqs):
+        to = lax.rem(s + d, seqs)
+        source = dw_ref.at[pl.ds(pl.multiple_of(to * slab_rows, slab_rows), slab_rows)]
+        w_waits.append(sender.copy(source, w_seq.at[d - 1], (to, c)))
+    move(dw_ref.at[pl.ds(pl.multiple_of(s * slab_rows, slab_rows), slab_rows)], w_mine)
+
+    vec_waits = []
+    for d in range(1, count):
+        to = (s, lax.rem(c + d, count))
+        for source, target in ((dsmall_ref, small_in), (db1_ref, b1_in), (db_ref, b_in)):
+            vec_waits.append(sender.copy(source, target.at[c], to))
+    small_in[c] = dsmall_ref[...]
+    b1_in[c] = db1_ref[...]
+    b_in[c] = db_ref[...]
+
+    for one in here:
+        one.wait()
+    for wait in dx_waits:
+        wait()
+    for k in range(chunks):
+        dx_sum[k] = added(dx_sum[k], *[dx_in[d, k] for d in range(repeat - 1)]).astype(bf16)
+    half_rows = rows // 2
+    token_lines = []
+    for h in range(2):
+        at = pl.ds(h * half_rows, half_rows)
+        token_lines.append(
+            Line(
+                sender, g, chunks, lambda to: (s, to * repeat + r),
+                lambda goal, at=at: (dx_sum.at[goal, at],),
+                lambda way, t, at=at: (dx_line.at[way, t, at],),
+            )
+        )
+    for line in token_lines:
+        line.send(0)
+
+    for wait in half_waits:
+        wait()
+    quarter = sum1.shape[0] // 4
+    for k in range(4):
+        at = slice(k * quarter, (k + 1) * quarter)
+        sum1[at] = added(sum1[at], in1[at]).astype(bf16)
+    quarter = sum2.shape[0] // 4
+    for k in range(4):
+        at = slice(k * quarter, (k + 1) * quarter)
+        sum2[at] = added(sum2[at], in2[at]).astype(bf16)
+    sum4[...] = added(sum4[...], in4[...]).astype(bf16)
+
+    def slab(seq):
+        at = pl.ds(pl.multiple_of(seq * slab_rows, slab_rows), slab_rows)
+        tall = pl.ds(pl.multiple_of(seq * slab_tall, slab_tall), slab_tall)
+        return sum1.at[at], sum2.at[tall], sum4.at[at]
+
+    masks = cube_steps(seqs, turn)
+
+    def family(seq, rest):
+        found = [seq]
+        for mask in rest:
+            found = found + [across(one, mask) for one in found]
+        return found
+
+    cube_waits, used = [], 0
+
+    def cube_send(j):
+        nonlocal used
+        partner = across(s, masks[j])
+        cube_waits.clear()
+        mine = family(s, masks[j + 1 :])
+        for k, seq in enumerate(family(partner, masks[j + 1 :])):
+            landing = cube1.at[used + k], cube2.at[used + k], cube4.at[used + k]
+            waits = [
+                sender.copy(source, target, (partner, c)) for source, target in zip(slab(seq), landing)
+            ]
+            cube_waits.append((mine[k], landing, waits))
+        used += len(cube_waits)
+
+    def cube_receive():
+        for seq, landing, waits in cube_waits:
+            for wait, target, arrived in zip(waits, slab(seq), landing):
+                wait()
+                target[...] = added(target[...], arrived[...]).astype(bf16)
+
+    cube_send(0)
+
+    for wait in w_waits:
+        wait()
+    w_mine[...] = added(w_mine[...], *[w_seq[d] for d in range(seqs - 1)]).astype(bf16)
+    w_waits = []
+    for d in range(1, blocks):
+        to = lax.rem(b + d, blocks)
+        source = w_mine.at[pl.ds(pl.multiple_of(to * block_rows, block_rows), block_rows)]
+        w_waits.append(sender.copy(source, w_block.at[b], (s, to * mates + i)))
+    w_block[b] = w_mine[pl.ds(pl.multiple_of(b * block_rows, block_rows), block_rows), :]
+
+    for wait in vec_waits:
+        wait()
+    vec_waits = []
+    small = small_in[0]
+    tall = b1_in[0]
+    for k in range(1, count):
+        small = small + small_in[k]
+        tall = tall + b1_in[k]
+    pair = []
+    for k in range(chunks):
+        one = b_in[k * repeat]
+        for d in range(1, repeat):
+            one = one + b_in[k * repeat + d]
+        pair.append(one)
+    for m in range(2):
+        joined = jnp.concatenate([one[0:1, m * width : (m + 1) * width] for one in pair], axis=1)
+        dsmall_out[6 + m : 7 + m, :] = joined
+    vec_seq[s, 0:6, 0:model] = small[0:6]
+    vec_seq[s, 6:8, 0:model] = dsmall_out[6:8, :]
+    vec_seq[s, :, model:] = tall
+    for d in range(1, seqs):
+        vec_waits.append(sender.copy(vec_seq.at[s], vec_seq.at[s], (lax.rem(s + d, seqs), c)))
+
+    for wait in w_waits:
+        wait()
+    w_waits = []
+    w_mates[i] = w_block[...]
+    for d in range(1, mates):
+        to = (s, b * mates + lax.rem(i + d, mates))
+        w_waits.append(sender.copy(w_block, w_mates.at[i], to))
+
+    def block_slab(goal):
+        row = s * slab_rows + goal * block_rows
+        tall = s * slab_tall + goal * block_tall
+        at = pl.ds(pl.multiple_of(row, block_rows), block_rows)
+        tall_at = pl.ds(pl.multiple_of(tall, block_tall), block_tall)
+        return sum1.at[at], sum2.at[tall_at], sum4.at[at]
+
+    weight_line = Line(
+        sender, b, blocks, lambda to: (s, to * mates + i),
+        block_slab, lambda way, t: (line1.at[way, t], line2.at[way, t], line4.at[way, t]),
+    )
+    steps = len(masks)
+    token_steps, weight_steps = chunks - 1, blocks - 1
+    for t in range(max(token_steps, steps + weight_steps)):
+        if t < token_steps:
+            for line in token_lines:
+                line.receive(t)
+                if t + 1 < token_steps:
+                    line.send(t + 1)
+        if t < steps:
+            cube_receive()
+            if t + 1 < steps:
+                cube_send(t + 1)
+            elif weight_steps:
+                weight_line.send(0)
+        elif t - steps < weight_steps:
+            weight_line.receive(t - steps)
+            if t - steps + 1 < weight_steps:
+                weight_line.send(t - steps + 1)
+
+    last_waits = []
+    for source, target in zip(block_slab(b), (last1, last2, last4)):
+        target[i] = source[...]
+        for d in range(1, mates):
+            to = (s, b * mates + lax.rem(i + d, mates))
+            last_waits.append(sender.copy(source, target.at[i], to))
+    dx_out[...] = dx_sum[g]
+    for wait in w_waits + vec_waits + last_waits:
+        wait()
+    for target, source in ((dw1_out, last1), (dw2_out, last2), (dwo_out, last4)):
+        size = target.shape[1] // 2
+        for which in range(2):
+            target[:, which * size : (which + 1) * size] = added(
+                *[source[k] for k in range(which, mates, 2)]
+            )
+    for k in range(chunks):
+        terms = [
+            w_mates[p, q]
+            for p in range(mates)
+            for q in range(blocks)
+            if (q * mates + p) // repeat == k
+        ]
+        dw_out[k] = added(*terms)
+    vec = vec_seq[0]
+    for d in range(1, seqs):
+        vec = vec + vec_seq[d]
+    dsmall_out[...] = vec[:, 0:model]
+    db1_out[...] = vec[:, model:]
+    sender.finish()
+
+
+def settle(dx, dw, dwo, dw1, dw2, dsmall, db1, db, chunks):
+    seqs, count = lax.axis_size("seq"), lax.axis_size("ctx")
+    _, rows, model = dx.shape
+    wide, tall = dw1.shape[1], dw2.shape[0]
+    devices = seqs * count
+    mates = block_mates(model // devices)
+    blocks, repeat = count // mates, count // chunks
+    block_rows, block_tall = mates * (model // devices), mates * (tall // devices)
+    slab_rows, slab_tall = blocks * block_rows, blocks * block_tall
+    padded = dw.shape[1]
+    semaphores = (
+        chunks * (repeat - 1) + 3 + (seqs - 1) + 3 * (count - 1) + 4 * (chunks - 1)
+        + 3 * (seqs - 1) + (blocks - 1) + (seqs - 1) + (mates - 1) + 6 * (blocks - 1) + 3 * (mates - 1)
+    )
+    shape = jax.ShapeDtypeStruct
+    f32, bf16 = jnp.float32, jnp.bfloat16
+    vmem, far = pl.BlockSpec(memory_space=pltpu.VMEM), pl.BlockSpec(memory_space=pl.ANY)
+    half_wide, half_model = wide // 2, model // 2
+    triple = lambda lead, a, t: [
+        pltpu.VMEM(lead + (a, half_wide), bf16),
+        pltpu.VMEM(lead + (t, half_model), bf16),
+        pltpu.VMEM(lead + (a, half_model), bf16),
+    ]
+    return pl.pallas_call(
+        partial(settle_kernel, seqs, count, chunks),
+        out_shape=(
+            shape((rows, model), bf16),
+            shape((chunks, block_rows, padded), f32),
+            shape((block_rows, model), f32),
+            shape((block_rows, wide), f32),
+            shape((block_tall, model), f32),
+            shape((8, model), f32),
+            shape((8, wide), f32),
+        ),
+        in_specs=[far] * 5 + [vmem] * 3,
+        out_specs=(vmem,) * 7,
+        scratch_shapes=[
+            pltpu.VMEM((chunks, rows, model), bf16),
+            pltpu.VMEM((repeat - 1, chunks, rows, model), bf16),
+            pltpu.VMEM((2, chunks - 1, rows, model), bf16),
+        ]
+        + triple((), model, tall)
+        + triple((), model, tall)
+        + triple((seqs - 1,), slab_rows, slab_tall)
+        + triple((2, blocks - 1), block_rows, block_tall)
+        + triple((mates,), block_rows, block_tall)
+        + [
+            pltpu.VMEM((slab_rows, padded), bf16),
+            pltpu.VMEM((seqs - 1, slab_rows, padded), bf16),
+            pltpu.VMEM((blocks, block_rows, padded), bf16),
+            pltpu.VMEM((mates, blocks, block_rows, padded), bf16),
+            pltpu.VMEM((8, 128), f32),
+            pltpu.VMEM((count, 8, model), f32),
+            pltpu.VMEM((count, 8, wide), f32),
+            pltpu.VMEM((count, 8, db.shape[1]), f32),
+            pltpu.VMEM((seqs, 8, model + wide), f32),
+            pltpu.SemaphoreType.DMA((semaphores,)),
+            pltpu.SemaphoreType.DMA((semaphores,)),
+            pltpu.SemaphoreType.DMA((chunks + 4,)),
+        ],
+        compiler_params=pltpu.CompilerParams(
+            vmem_limit_bytes=VMEM_LIMIT, collective_id=2, has_side_effects=True
+        ),
+        name="settle",
+    )(dx, dw, dwo, dw1, dw2, dsmall, db1, db)
+
+
+def swap_kernel(chunks, repeat, a_ref, a_out, send_sems, recv_sems, here_sem):
+    s, c = lax.axis_index("seq"), lax.axis_index("ctx")
+    g, r = c // repeat, lax.rem(c, repeat)
+    place = lambda d: lax.rem(g + d, chunks)
+    barrier = pltpu.get_barrier_semaphore()
+    for d in range(1, chunks):
+        pl.semaphore_signal(
+            barrier, inc=1, device_id=(s, place(d) * repeat + r), device_id_type=MESH
+        )
+    pl.semaphore_wait(barrier, chunks - 1)
+    sender = Sender(send_sems, recv_sems)
+    here = pltpu.make_async_copy(a_ref.at[g], a_out.at[g], here_sem)
+    here.start()
+    waits = [
+        sender.copy(a_ref.at[place(d)], a_out.at[g], (s, place(d) * repeat + r))
+        for d in range(1, chunks)
+    ]
+    for wait in waits:
+        wait()
+    here.wait()
+    sender.finish()
+
+
+def swap(a):
+    chunks = a.shape[0]
+    far = pl.BlockSpec(memory_space=pl.ANY)
+    return pl.pallas_call(
+        partial(swap_kernel, chunks, lax.axis_size("ctx") // chunks),
+        out_shape=jax.ShapeDtypeStruct(a.shape, a.dtype),
+        in_specs=[far],
+        out_specs=far,
+        scratch_shapes=[
+            pltpu.SemaphoreType.DMA((chunks - 1,)),
+            pltpu.SemaphoreType.DMA((chunks - 1,)),
+            pltpu.SemaphoreType.DMA,
+        ],
+        compiler_params=pltpu.CompilerParams(collective_id=3, has_side_effects=True),
+        name="swap",
+    )(a)
+
+
+def pick(values, size, device):
+    wide = values.shape[1]
+    row = lax.broadcasted_iota(jnp.int32, (wide, size), 0)
+    column = lax.broadcasted_iota(jnp.int32, (wide, size), 1)
+    chosen = (row == column + device * size).astype(jnp.bfloat16)
+    high = values.astype(jnp.bfloat16)
+    rest = values - high.astype(jnp.float32)
+    middle_part = rest.astype(jnp.bfloat16)
+    low = (rest - middle_part.astype(jnp.float32)).astype(jnp.bfloat16)
+    return nn(high, chosen) + nn(middle_part, chosen) + nn(low, chosen)
+
+
+def finish_kernel(
+    count, mates,
+    e1_ref, dx_ref, dw_ref, dwo_ref, dw1_ref, dw2_ref, small_ref, b1_ref,
+    dx_out, dwq_out, dwk_out, dwv_out, dwo_out, dw1_out, dw2_out, small_out, b1_out,
+):
+    s, c = lax.axis_index("seq"), lax.axis_index("ctx")
+    dx_out[...] = e1_ref[...] + dx_ref[...].astype(jnp.float32)
+    each, tall = dwo_out.shape[0], dw2_out.shape[0]
+    chunks = dw_ref.shape[0]
+    width = dwq_out.shape[1] // chunks
+    i = lax.rem(c, mates)
+    for p in range(mates):
+        rows = slice(p * each, (p + 1) * each)
+
+        @pl.when(i == p)
+        def _():
+            for m, out in enumerate((dwq_out, dwk_out, dwv_out)):
+                parts = [dw_ref[k, rows, m * width : (m + 1) * width] for k in range(chunks)]
+                out[...] = jnp.concatenate(parts, axis=1)
+            dwo_out[...] = dwo_ref[rows, :]
+            dw1_out[...] = dw1_ref[rows, :]
+            dw2_out[...] = dw2_ref[p * tall : (p + 1) * tall, :]
+
+    device = s * count + c
+    small_out[...] = pick(small_ref[...], each, device)
+    b1_out[...] = pick(b1_ref[...], tall, device)
+
+
+def finish(e1, dx, dw, dwo, dw1, dw2, small, b1):
+    count = lax.axis_size("ctx")
+    devices = count * lax.axis_size("seq")
+    model, wide = dwo.shape[1], dw1.shape[1]
+    each, tall = model // devices, wide // devices
+    shape = jax.ShapeDtypeStruct
+    f32 = jnp.float32
+    vmem = pl.BlockSpec(memory_space=pltpu.VMEM)
+    return pl.pallas_call(
+        partial(finish_kernel, count, block_mates(each)),
+        out_shape=(shape(e1.shape, f32),)
+        + (shape((each, model), f32),) * 4
+        + (shape((each, wide), f32), shape((tall, model), f32), shape((8, each), f32), shape((8, tall), f32)),
+        in_specs=[vmem] * 8,
+        out_specs=(vmem,) * 9,
+        compiler_params=pltpu.CompilerParams(vmem_limit_bytes=VMEM_LIMIT),
+        name="finish",
+    )(e1, dx, dw, dwo, dw1, dw2, small, b1)
 
 
 def on_device(
@@ -581,67 +1413,31 @@
     output_weight, output_bias, attn_norm_gain, attn_norm_shift, up_weight, up_bias, down_weight,
     down_bias, ffn_norm_gain, ffn_norm_shift, out_cotangent,
 ):
-    both = ("seq", "ctx")
-    bf16 = jnp.bfloat16
     count = lax.axis_size("ctx")
     chunks = math.gcd(H, count)
-    repeat = count // chunks
     heads = H // chunks
-    width = heads * DH
     x = tokens[0]
-    rows, model = x.shape
-    group = lax.axis_index("ctx") // repeat
-
-    def gather(a):
-        return lax.all_gather(a.astype(bf16), both, axis=0, tiled=True)
-
-    def share(a):
-        return lax.dynamic_slice_in_dim(a, group * width, width, a.ndim - 1)
-
-    wq, wk, wv = gather(query_weight), gather(key_weight), gather(value_weight)
-    wo, w1, w2 = gather(output_weight), gather(up_weight), gather(down_weight)
-    small_parts = (output_bias, attn_norm_gain, attn_norm_shift, down_bias, ffn_norm_gain, ffn_norm_shift)
-    small = [gather(a).astype(jnp.float32) for a in small_parts]
-    small = jnp.stack(small + [jnp.zeros_like(small[0])] * 2)
-    b1 = jnp.broadcast_to(gather(up_bias).astype(jnp.float32)[None], (8, up_bias.shape[0] * lax.axis_size(both)))
-    bias = jnp.concatenate([share(gather(query_bias)), share(gather(value_bias))]).astype(jnp.float32)
-    bias = jnp.broadcast_to(bias[:, None], (2 * width, LANES))
-    padded = -(-3 * width // LANES) * LANES
-    w = jnp.concatenate(
-        [share(wq), share(wk), share(wv), jnp.zeros((model, padded - 3 * width), bf16)], axis=1
+    vec = jnp.concatenate([
+        output_bias, attn_norm_gain, attn_norm_shift, down_bias, ffn_norm_gain, ffn_norm_shift,
+        query_bias, value_bias, up_bias,
+    ])
+    vec = jnp.pad(vec, (0, -vec.shape[0] % LANES))[None]
+    w, wo, w1, w2, x_all, codes, vecs = collect(
+        query_weight, key_weight, value_weight, output_weight, up_weight, down_weight,
+        x, segment_ids * 2 + valid_tokens, vec, chunks,
     )
-    x_all = lax.all_gather(x, "ctx", axis=0, tiled=True)
-    seg = lax.all_gather(segment_ids[0], "ctx", axis=0)
-    val = lax.all_gather(valid_tokens[0], "ctx", axis=0)
-    k, v, q, o_float, o_send, lse = attend(x_all, w, bias, seg, val, heads, chunks)
-    groups = [[g * repeat + r for g in range(chunks)] for r in range(repeat)]
-
-    def exchange(a):
-        return lax.all_to_all(a, "ctx", 0, 0, axis_index_groups=groups, tiled=True)
-
+    k, v, q, o_float, o_send, lse, codes = attend(x_all, w, vecs, codes, heads, chunks)
     output, e1, do, dwo, dw1, dw2, dsmall, db1 = middle(
-        exchange(o_send), x, out_cotangent[0], wo, w1, w2, small, b1
+        swap(o_send), x, out_cotangent[0], wo, w1, w2, vecs
     )
-    dx, dw, db = retreat(x_all, w, k, v, q, o_float, lse, exchange(do), seg, val, heads, chunks)
-    dx = lax.psum_scatter(dx, "ctx", scatter_dimension=0, tiled=True)[0]
-
-    def place(a, wide):
-        return lax.dynamic_update_slice_in_dim(
-            jnp.zeros(a.shape[:-1] + (wide,), a.dtype), a, group * width, a.ndim - 1
-        )
-
-    def scatter(a):
-        return lax.psum_scatter(a, both, scatter_dimension=0, tiled=True).astype(jnp.float32)
-
-    dwq, dwk, dwv = [scatter(place(dw[:, i * width : (i + 1) * width], model)) for i in range(3)]
-    dbq, dbv = [scatter(place(db[0, i * width : (i + 1) * width], model)) for i in range(2)]
-    dbo, dg1, dc1, db2, dg2, dc2 = [scatter(dsmall[i]) for i in range(6)]
+    dx, dw, db = retreat(x_all, w, k, v, q, o_float, lse, swap(do), codes, heads, chunks)
+    summed = settle(dx, dw, dwo, dw1, dw2, dsmall, db1, db, chunks)
+    grad, dwq, dwk, dwv, dwo, dw1, dw2, small, b1 = finish(e1, *summed)
     return (
-        output[None],
-        (e1 + dx.astype(jnp.float32))[None],
-        dwq, dbq, dwk, dwv, dbv,
-        scatter(dwo), dbo, dg1, dc1,
-        scatter(dw1), scatter(db1[0]), scatter(dw2), db2, dg2, dc2,
+        output[None], grad[None],
+        dwq, small[6], dwk, dwv, small[7],
+        dwo, small[0], small[1], small[2],
+        dw1, b1[0], dw2, small[3], small[4], small[5],
     )
 
 

time: 1190 us -> 431 us (0.36)
  waiting for transfers between devices: 811 us -> 0 us
  Pallas kernels: 173 us -> 424 us
  blocking collectives: 134 us -> 0 us
  local copies, waits for them, and re-layouts: 34.5 us -> 4.14 us
  other arithmetic: 20.3 us -> 1.28 us
  between operations: 14.5 us -> 0.89 us
    reduce_scatter x7 -> x0, waiting for transfers between devices: 519 us -> none  [the longest x6 450 us: scatter(): lax.psum_scatter(a, both, scatter_dimension=0, tiled=True)]
    all_gather x7 -> x0, waiting for transfers between devices: 289 us -> none  [the longest x6 226 us: gather(): return lax.all_gather(a.astype(bf16), both, axis=0, tiled=True)]
    pallas_call x0 -> x5, Pallas kernels: none -> 250 us  [the longest x1 109 us: settle(): pl.pallas_call(partial(settle_kernel, seqs, count, chunks), out_shape=(sh...]
    unnamed x2 -> x0, blocking collectives: 84.3 us -> none
    all_gather x2 -> x0, blocking collectives: 25.4 us -> none  [the longest x1 12.7 us: on_device(): seg = lax.all_gather(segment_ids[0], 'ctx', axis=0)]
    all_to_all x1 -> x0, blocking collectives: 23.9 us -> none  [exchange(): return lax.all_to_all(a, 'ctx', 0, 0, axis_index_groups=groups, tiled=True)]
    convert_element_type x22 -> x0, other arithmetic: 16.5 us -> none  [the longest x6 8.91 us: scatter(): lax.psum_scatter(a, both, scatter_dimension=0, tiled=True)]
    unnamed x69 -> x0, local copies, waits for them, and re-layouts: 12.8 us -> none
  transfers between devices with their start and end apart: 15 -> 0, of which waited for: 12 -> 0; matrix products, arithmetic and copies ran while one was open for 4% -> 0% of each run, Pallas kernels for 11% -> 0%
where the time goes in v2:
time: 431 us
  Pallas kernels  424 us (98%)
    pallas_call x1, Pallas kernels, settle(): pl.pallas_call(partial(settle_kernel, seqs, count, chunks), out_shape=(sh...  109 us
    pallas_call x1, Pallas kernels, collect(): pl.pallas_call(partial(collect_kernel, seqs, count, chunks, semaphores),...  100 us
    pallas_call x1, Pallas kernels, retreat(): pl.pallas_call(partial(retreat_kernel, heads, chunks, 'ctx', repeat), out...  85.8 us
    pallas_call x1, Pallas kernels, attend(): pl.pallas_call(partial(attend_kernel, heads, chunks, 'ctx', repeat), out_...  50.3 us
    pallas_call x1, Pallas kernels, middle(): pl.pallas_call(middle_kernel, out_shape=(shape((rows, model), f32), shape...  37.9 us
    pallas_call x2, Pallas kernels, swap(): pl.pallas_call(partial(swap_kernel, chunks, lax.axis_size('ctx') // chunk...  37.6 us

profile of v2, /device:TPU:0, one launch (start us, length us, event | category | flops | bytes accessed | tf_op | source)
XLA Modules:
  0.0 430.5 jit_solution(8997186578438653351)
XLA Ops:
  0.7 1.3 multiply_add_fusion.code_ref
  1.9 0.9 concatenate.3
  2.8 0.6 broadcast_in_dim.9.vec_ref
  3.4 100.2 %collect.1 = (bf16[768,640]{1,0:T(8,128)(2,1)}, bf16[768,768]{1,0:T(8,128)(2,1)}, bf16[768,3072]{1,0:T(8,128)(2,1)}, bf16[3072,768]{1,0:T(8,128)(2,1)}, bf16[409...) custom-call(f32[24,768]{1,0:T(8,128)} %wq_ref.1, f32[24,768]{1,0:T(8,128)} %wk_ref.1, ...), custom_call_target="tpu_custom_call" | custom-call | tf_op jit(solution)/shard_map/collect/pallas_call | solution.py:926
  103.6 50.3 %attend.1 = (bf16[3,4864,64]{2,1,0:T(8,128)(2,1)}, bf16[192,4096]{1,0:T(8,128)(2,1)}, bf16[192,2048]{1,0:T(8,128)(2,1)}, f32[192,2048]{1,0:T(8,128)}, bf16[4,192...) custom-call(bf16[4096,768]{1,0:T(8,128)(2,1)} %get-tuple-element.58.x_ref, ...), custom_call_target="tpu_custom_call" | custom-call | tf_op jit(solution)/shard_map/attend/pallas_call | solution.py:217
  153.9 17.5 %swap.2.o_ref = bf16[4,192,512]{2,1,0:T(8,128)(2,1)} custom-call(bf16[4,192,512]{2,1,0:T(8,128)(2,1)} %get-tuple-element.62.a_ref), custom_call_target="tpu_custom_call" | custom-call | tf_op jit(solution)/shard_map/swap/pallas_call | solution.py:1336
  171.4 37.9 %middle.1 = (f32[512,768]{1,0:T(8,128)}, f32[512,768]{1,0:T(8,128)}, bf16[4,192,512]{2,1,0:T(8,128)(2,1)}, bf16[768,768]{1,0:T(8,128)(2,1)}, bf16[768,3072]{1,0:...) custom-call(bf16[4,192,512]{2,1,0:T(8,128)(2,1)} %swap.2.o_ref, ...), custom_call_target="tpu_custom_call" | custom-call | tf_op jit(solution)/shard_map/middle/pallas_call | solution.py:586
  209.2 20.2 %swap.3.do_ref = bf16[4,192,512]{2,1,0:T(8,128)(2,1)} custom-call(bf16[4,192,512]{2,1,0:T(8,128)(2,1)} %get-tuple-element.73.a_ref), custom_call_target="tpu_custom_call" | custom-call | tf_op jit(solution)/shard_map/swap/pallas_call | solution.py:1336
  229.4 85.8 %retreat.1 = (bf16[8,512,768]{2,1,0:T(8,128)(2,1)}, bf16[768,640]{1,0:T(8,128)(2,1)}, f32[8,384]{1,0:T(8,128)}) custom-call(bf16[4096,768]{1,0:T(8,128)(2,1)} %get-tuple-element.58.x_ref, bf16[768,640]{1,0:T(8,128)(2,1)} %get-tuple-element.59.w_ref, bf16[3,4864,64]{2,1,0:T(8,128)(2,1)} %get-tuple-element.68.k_ref, ...), custom_call_target="tpu_custom_call" | custom-call | tf_op jit(solution)/shard_map/retreat/pallas_call | solution.py:443
  315.2 108.6 %settle.1 = (bf16[512,768]{1,0:T(8,128)(2,1)}, f32[4,48,640]{2,1,0:T(8,128)}, f32[48,768]{1,0:T(8,128)}, f32[48,3072]{1,0:T(8,128)}, f32[192,768]{1,0:T(8,128)}, /*index=5*/f32[8,768]{1,0:T(8,128)}, f32[8,3072]{1,0:T(8,128)}) custom-call(bf16[8,512,768]{2,1,0:T(8,128)(2,1)} %get-tuple-element.75.dx_ref, bf16[768,640]{1,0:T(8,128)(2,1)} %get-tuple-element.76.dw_ref, ...), custom_call_target="tpu_custom_call" | custom-call | tf_op jit(solution)/shard_map/settle/pallas_call | solution.py:1266
  423.8 3.9 finish.1
  427.7 1.2 slice_bitcast_fusion.3
  428.8 1.5 slice_bitcast_fusion
  (1 shorter events, 0.0 us)
